TPU v7x, 256 devices: a whole 4x4x8 slice. The times are simulated.
256 devices in a mesh: st: 32 (over x, y, core), ha: 8 (over z).
Axes of the slice: x: 4, y: 4, z: 8, core: 2. Of those that a mesh axis runs over, the one named last changes fastest.
Arguments:
- clip_lengths: int32 [4], replicated, may hold values from 1 to 32, 64 in all
- inst_frame: int32 [4096, 1], P('st'), may hold values from 0 to 63; in each aligned block of 128 rows (0 to 127, 128 to 255, ...) at most 4 rows name the same one
- query_rows: int32 [4096], P('st'), may hold values from 1 to 16
- pix_q: bfloat16 [64, 256, 64, 128], P('st', 'ha'), may hold values from -140 to 140
- pix_k: bfloat16 [64, 256, 64, 128], P('st', 'ha'), may hold values from -4.5 to 4.5
- pix_v: bfloat16 [64, 256, 64, 128], P('st', 'ha'), may hold values from -6 to 6
- features: bfloat16 [64, 256, 64, 128], P('st', 'ha'), may hold values from -4 to 4
- pixel_gain: float32 [256], P('ha'), may hold values from 0.1 to 1.9
- inst_query: bfloat16 [4096, 16, 256], P('st', None, 'ha'), may hold values from -135 to 135
- inst_gain: float32 [256], P('ha'), may hold values from 0.1 to 1.9
Outputs:
- pixel_out: bfloat16 [64, 256, 64, 128], P('st', 'ha')
- inst_out: bfloat16 [4096, 16, 256], P('st', None, 'ha')
Inputs may be any that keep to these rules, and one draw needn't show every extreme that they name: `clip_lengths`: the clips lie end to end in frame order and their lengths sum to 64. `inst_frame`: among the instances held by one index of st, no frame is named by more than 4 instances.
All inputs are finite; a program needn't handle non-finite values.
Results may differ from a plain program's by a relative error of at most 0.012.
Values may be sent and summed in bfloat16 or wider, within the bound.
A program may use at most 64 MiB of HBM per device.

v0:
```python
from functools import partial
import math

import jax
import jax.numpy as jnp
from jax import lax
from jax.sharding import PartitionSpec as P

C = 256
HD = 32


EPSILON = 1e-05
MASKED = -1e30


def soft_weights(scores, axis_num):
    largest = jnp.max(scores, axis=axis_num, keepdims=True)
    raised = jnp.exp(scores - largest)
    return (raised / jnp.sum(raised, axis=axis_num, keepdims=True)).astype(jnp.bfloat16)


def spatial_frame(inputs):
    query_f, key_f, value_f = inputs
    channels, rows_n, cols_n = query_f.shape
    heads_n = channels // HD
    scale_val = HD ** (-0.5)
    query_h = query_f.reshape(heads_n, HD, rows_n, cols_n)
    key_h = key_f.reshape(heads_n, HD, rows_n, cols_n)
    value_h = value_f.reshape(heads_n, HD, rows_n, cols_n)
    height_scores = (
        jnp.einsum("ndhw,ndgw->nhgw", query_h, key_h, preferred_element_type=jnp.float32)
        * scale_val
    )
    height_weights = soft_weights(height_scores, 2)
    height_out = jnp.einsum(
        "nhgw,ndgw->ndhw", height_weights, value_h, preferred_element_type=jnp.float32
    )
    width_scores = (
        jnp.einsum("ndhw,ndhv->nhwv", query_h, key_h, preferred_element_type=jnp.float32)
        * scale_val
    )
    width_weights = soft_weights(width_scores, 3)
    width_out = jnp.einsum(
        "nhwv,ndhv->ndhw", width_weights, value_h, preferred_element_type=jnp.float32
    )
    return (height_out + width_out).reshape(channels, rows_n, cols_n)


def temporal_attend(same_clip, patch):
    query_p, key_p, value_p = patch
    frames_n, channels, rows_n, cols_n = query_p.shape
    shape_heads = (frames_n, channels // HD, HD, rows_n, cols_n)
    scale_val = HD ** (-0.5)
    scores = (
        jnp.einsum(
            "fndpw,gndpw->nfgpw",
            query_p.reshape(shape_heads),
            key_p.reshape(shape_heads),
            preferred_element_type=jnp.float32,
        )
        * scale_val
    )
    masked = jnp.where(same_clip[None, :, :, None, None], scores, MASKED)
    weights = soft_weights(masked, 2)
    result = jnp.einsum(
        "nfgpw,gndpw->fndpw",
        weights,
        value_p.reshape(shape_heads),
        preferred_element_type=jnp.float32,
    )
    return result.astype(jnp.bfloat16).reshape(frames_n, channels, rows_n, cols_n)


def attend_block(key_h, value_h, query_block):
    scale_val = HD ** (-0.5)
    scores = (
        jnp.einsum("rnd,ndt->nrt", query_block, key_h, preferred_element_type=jnp.float32)
        * scale_val
    )
    weights = soft_weights(scores, 2)
    result = jnp.einsum("nrt,ndt->rnd", weights, value_h, preferred_element_type=jnp.float32)
    return result.astype(jnp.bfloat16).reshape(query_block.shape[0], -1)


def normalize(values_in, totals, squares, count_all, gain_vec):
    average = totals / count_all
    variance = squares / count_all - average * average
    return (values_in - average) * lax.rsqrt(variance + EPSILON) * gain_vec


def per_device(
    clip_lengths,
    inst_frame,
    query_rows,
    pix_q,
    pix_k,
    pix_v,
    features,
    pixel_gain,
    inst_query,
    inst_gain,
):
    st_count = lax.axis_size("st")
    frames_local = pix_q.shape[0]
    frame_total = frames_local * st_count
    clip_ends = jnp.cumsum(clip_lengths)
    frame_ids = jnp.arange(frame_total, dtype=jnp.int32)
    clip_of = jnp.sum((clip_ends[None, :] <= frame_ids[:, None]).astype(jnp.int32), axis=1)
    same_clip = clip_of[:, None] == clip_of[None, :]
    attend_time = partial(temporal_attend, same_clip)
    time_patch = attend_time(
        (
            lax.all_to_all(pix_q, "st", split_axis=2, concat_axis=0, tiled=True),
            lax.all_to_all(pix_k, "st", split_axis=2, concat_axis=0, tiled=True),
            lax.all_to_all(pix_v, "st", split_axis=2, concat_axis=0, tiled=True),
        )
    )
    temporal = lax.all_to_all(time_patch, "st", split_axis=0, concat_axis=2, tiled=True)
    spatial = lax.map(spatial_frame, (pix_q, pix_k, pix_v))
    inst_count, qmax_rows, channels = inst_query.shape
    frame_most = max(2, 2 * inst_count // frame_total)
    slot_total = frame_total * frame_most
    target = inst_frame[:, 0]
    same_target = target[:, None] == target[None, :]
    inst_ids = jnp.arange(inst_count, dtype=jnp.int32)
    earlier = inst_ids[None, :] < inst_ids[:, None]
    arrival = jnp.sum((same_target & earlier).astype(jnp.int32), axis=1)
    slot_id = target * frame_most + arrival
    placement_map = (jnp.arange(slot_total, dtype=jnp.int32)[:, None] == slot_id[None, :]).astype(
        jnp.bfloat16
    )
    send_rows = jnp.dot(
        placement_map,
        inst_query.reshape(inst_count, qmax_rows * channels),
        preferred_element_type=jnp.float32,
    )
    send_rows = send_rows.astype(jnp.bfloat16).reshape(
        st_count, frames_local, frame_most, qmax_rows, channels
    )
    received = lax.all_to_all(send_rows, "st", split_axis=0, concat_axis=0, tiled=True)
    sources, frames_n, items, query_count, chans_in = received.shape
    heads_n = chans_in // HD
    results = []
    for local_frame in range(frames_n):
        rows_all = received[:, local_frame].reshape(-1, heads_n, HD)
        row_count = rows_all.shape[0]
        block_rows = math.gcd(row_count, 256)
        blocks = rows_all.reshape(row_count // block_rows, block_rows, heads_n, HD)
        key_h = pix_k[local_frame].reshape(heads_n, HD, -1)
        value_h = pix_v[local_frame].reshape(heads_n, HD, -1)
        answered = lax.map(partial(attend_block, key_h, value_h), blocks)
        results.append(answered.reshape(sources, items, query_count, chans_in))
    answers = jnp.stack(results, axis=1)
    returned = lax.all_to_all(answers, "st", split_axis=0, concat_axis=0, tiled=True)
    returned = returned.reshape(slot_total, qmax_rows * channels)
    own_rows = lax.dot_general(
        placement_map, returned, (((0,), (0,)), ((), ())), preferred_element_type=jnp.float32
    )
    own_rows = own_rows.reshape(inst_count, qmax_rows, channels)
    pixel_pre = features.astype(jnp.float32) + spatial + temporal.astype(jnp.float32)
    pixel_totals = jnp.sum(pixel_pre, axis=1)
    pixel_squares = jnp.sum(pixel_pre * pixel_pre, axis=1)
    inst_pre = inst_query.astype(jnp.float32) + own_rows
    inst_totals = jnp.sum(inst_pre, axis=2)
    inst_squares = jnp.sum(inst_pre * inst_pre, axis=2)
    pixel_totals, pixel_squares = (
        lax.psum(pixel_totals.astype(jnp.bfloat16), "ha").astype(jnp.float32),
        lax.psum(pixel_squares.astype(jnp.bfloat16), "ha").astype(jnp.float32),
    )
    inst_totals, inst_squares = lax.psum((inst_totals, inst_squares), "ha")
    pixel_out = normalize(
        pixel_pre, pixel_totals[:, None], pixel_squares[:, None], C, pixel_gain[None, :, None, None]
    ).astype(jnp.bfloat16)
    normed = normalize(inst_pre, inst_totals[:, :, None], inst_squares[:, :, None], C, inst_gain)
    valid = jnp.arange(qmax_rows, dtype=jnp.int32)[None, :] < query_rows[:, None]
    inst_out = jnp.where(valid[:, :, None], normed, 0.0).astype(jnp.bfloat16)
    return (pixel_out, inst_out)


def solution(mesh):
    placed = (
        P(),
        P("st", None),
        P("st"),
        P("st", "ha", None, None),
        P("st", "ha", None, None),
        P("st", "ha", None, None),
        P("st", "ha", None, None),
        P("ha"),
        P("st", None, "ha"),
        P("ha"),
    )
    return jax.shard_map(
        per_device,
        mesh=mesh,
        in_specs=placed,
        out_specs=(P("st", "ha", None, None), P("st", None, "ha")),
        check_vma=False,
    )
```

profile of v0, /device:TPU:14, one launch (start us, length us, event | category | flops | bytes accessed | tf_op | source)
XLA Modules:
  0.0 359.0 jit_solution(12869337177136443340)
XLA Ops:
  10.6 1.6 reshape.286
  12.1 3.1 reshape.291
  15.2 7.5 %all-to-all-start.4 = ((bf16[32,2,2048]{2,1,0:T(2,128)(2,1)}), bf16[32,2,2048]{2,1,0:T(2,128)(2,1)S(1)}, u32[]{:S(2)}, u32[]{:S(2)}) async-start(bf16[32,2,2048]{2,1,0:T(2,128)(2,1)} %reshape.291), calls=%async_computation.4 | async-start | bytes 524288 | tf_op jit(solution)/shard_map/all_to_all | solution.py:141
  22.7 1.6 copy.132
  24.6 1.7 copy.124
  26.2 1.7 copy.127
  28.4 7.8 %all-to-all-start.2 = ((bf16[2,32,64,128]{3,1,0,2:T(8,128)(2,1)}), bf16[2,32,64,128]{3,1,0,2:T(8,128)(2,1)}, u32[]{:S(2)}, u32[]{:S(2)}) async-start(bf16[2,32,64,128]{3,1,0,2:T(8,128)(2,1)} %copy.132), calls=%async_computation.2 | async-start | bytes 2097152 | tf_op jit(solution)/shard_map/all_to_all | solution.py:116
  40.6 9.4 %all-to-all-done.2 = bf16[2,32,64,128]{3,1,0,2:T(8,128)(2,1)} async-done(((bf16[2,32,64,128]{3,1,0,2:T(8,128)(2,1)}), bf16[2,32,64,128]{3,1,0,2:T(8,128)(2,1)}, u32[]{:S(2)}, u32[]{:S(2)}) %all-to-all-start.2) | async-done | bytes 1048608 | tf_op jit(solution)/shard_map/all_to_all | solution.py:116
  50.1 7.4 %all-to-all-start = ((bf16[2,32,64,128]{3,1,0,2:T(8,128)(2,1)}), bf16[2,32,64,128]{3,1,0,2:T(8,128)(2,1)S(1)}, u32[]{:S(2)}, u32[]{:S(2)}) async-start(bf16[2,32,64,128]{3,1,0,2:T(8,128)(2,1)} %copy.124), calls=%async_computation | async-start | bytes 2097152 | tf_op jit(solution)/shard_map/all_to_all | solution.py:115
  57.5 33.8 %while.32 = (s32[]{:T(128)}, bf16[8,256,32]{1,2,0:T(8,128)(2,1)S(1)}, bf16[8,256,1,32]{1,3,2,0:T(8,128)(2,1)S(1)}, bf16[1,32,8192]{2,1,0:T(8,128)(2,1)S(1)}, bf16[1,32,8192]{2,1,0:T(8,128)(2,1)}, /*index=5*/s32[]{:T(128)}) while((s32[]{:T(128)}, bf16[8,256,32]{1,2,0:T(8,128)(2,1)S(1)}, bf16[8,256,1,32]{1,3,2,0:T(8,128)(2,1)S(1)}, ...), condition=%wide.region_22.23_spmd, body=%wide.region_19.22_spmd.sunk | while | flops 283123200 | bytes 28349552 | solution.py:152
  91.4 7.5 %all-to-all-start.1 = ((bf16[2,32,64,128]{3,1,0,2:T(8,128)(2,1)}), bf16[2,32,64,128]{3,1,0,2:T(8,128)(2,1)}, u32[]{:S(2)}, u32[]{:S(2)}) async-start(bf16[2,32,64,128]{3,1,0,2:T(8,128)(2,1)} %copy.127), calls=%async_computation.1 | async-start | bytes 2097152 | tf_op jit(solution)/shard_map/all_to_all | solution.py:114
  98.9 33.8 %while.31 = (s32[]{:T(128)}, bf16[8,256,32]{1,2,0:T(8,128)(2,1)S(1)}, bf16[8,256,1,32]{1,3,2,0:T(8,128)(2,1)S(1)}, bf16[1,32,8192]{2,1,0:T(8,128)(2,1)S(1)}, bf16[1,32,8192]{2,1,0:T(8,128)(2,1)S(1)}, /*index=5*/s32[]{:T(128)}) while((s32[]{:T(128)}, bf16[8,256,32]{1,2,0:T(8,128)(2,1)S(1)}, bf16[8,256,1,32]{1,3,2,0:T(8,128)(2,1)S(1)}, ...), condition=%wide.region_18.19_spmd, body=%wide.region_15.18_spmd.sunk | while | flops 283123200 | bytes 26252372 | solution.py:152
  101.7 1.5 fusion.102
  110.1 1.5 fusion.102
  114.3 1.5 fusion.102
  118.6 1.5 fusion.102
  127.0 1.5 fusion.102
  133.8 1.7 reshape.293
  136.9 4.4 %copy.136 = bf16[64,32,2,128]{0,1,3,2:T(8,128)(2,1)} copy(bf16[64,32,2,128]{3,1,2,0:T(8,128)(2,1)S(1)} %bitcast.211) | data formatting | bytes 2097152 | tf_op jit(solution)/shard_map/reshape.63
  141.4 3.4 copy.130
  144.9 7.7 %all-to-all-start.5 = ((bf16[32,2,2048]{2,1,0:T(2,128)(2,1)}), bf16[32,2,2048]{2,1,0:T(2,128)(2,1)S(1)}, u32[]{:S(2)}, u32[]{:S(2)}) async-start(bf16[32,2,2048]{2,1,0:T(2,128)(2,1)} %reshape.293), calls=%async_computation.5 | async-start | bytes 524288 | tf_op jit(solution)/shard_map/all_to_all | solution.py:155
  153.9 4.3 %copy.131 = bf16[64,32,2,128]{0,1,3,2:T(8,128)(2,1)} copy(bf16[64,32,2,128]{3,1,2,0:T(8,128)(2,1)S(1)} %bitcast.213) | data formatting | bytes 2097152 | tf_op jit(solution)/shard_map/reshape.59
  158.2 3.6 %fusion.44 = (f32[64,2,128]{0,2,1:T(8,128)S(1)}, f32[2,128,64,64]{3,2,1,0:T(8,128)S(1)}) fusion(pred[64,64]{0,1:T(8,128)(4,1)S(1)} %copy-done.12, bf16[64,32,2,128]{0,1,3,2:T(8,128)(2,1)S(1)} %copy.130, bf16[64,32,2,128]{0,1,3,2:T(8,128)(2,1)} %copy.131), kind=kOutput, calls=%fused_computation.60 | convolution fusion | flops 70238208 | bytes 6361088 | tf_op jit(solution)/shard_map/fndpw,gndpw->nfgpw/dot_general | solution.py:56
  161.9 3.0 fusion.43
  164.9 2.2 convert_bitcast_fusion.1
  167.1 3.9 %copy.137 = bf16[64,32,2,128]{3,1,2,0:T(8,128)(2,1)} copy(bf16[64,32,2,128]{0,1,3,2:T(8,128)(2,1)S(1)} %convert_bitcast_fusion.1) | data formatting | bytes 2097152 | tf_op jit(solution)/shard_map/reshape | solution.py:72
  171.0 7.4 %all-to-all-start.3 = ((bf16[64,32,2,128]{3,1,2,0:T(8,128)(2,1)}), bf16[64,32,2,128]{3,1,2,0:T(8,128)(2,1)}, u32[]{:S(2)}, u32[]{:S(2)}) async-start(bf16[64,32,2,128]{3,1,2,0:T(8,128)(2,1)} %copy.137), calls=%async_computation.3 | async-start | bytes 2097152 | tf_op jit(solution)/shard_map/all_to_all | solution.py:119
  178.9 59.9 %while.30 = (s32[]{:T(128)}, f32[2,32,64,128]{3,1,2,0:T(8,128)}, bf16[2,32,64,128]{3,2,1,0:T(8,128)(2,1)}, bf16[2,32,64,128]{3,2,1,0:T(8,128)(2,1)}, bf16[2,32,64,128]{3,2,1,0:T(8,128)(2,1)}, /*index=5*/s32[]{:T(128)}) while((s32[]{:T(128)}, f32[2,32,64,128]{3,1,2,0:T(8,128)}, bf16[2,32,64,128]{3,2,1,0:T(8,128)(2,1)}, ...), condition=%wide.region_5.6_spmd, body=%wide.region_0.5_spmd.sunk | while | flops 212582528 | bytes 59998384 | solution.py:120
  181.0 3.7 %fusion.95 = (f32[64,128]{1,0:T(8,128)S(1)}, f32[64,128,128]{1,2,0:T(8,128)S(1)}) fusion(f32[64,128,128]{1,2,0:T(8,128)S(1)} %fusion.94), kind=kOutput, calls=%fused_computation.94.clone.1 | output fusion | flops 4194431 | bytes 8421376 | tf_op jit(solution)/shard_map/while/body/eval_jaxpr/sub | solution.py:19
  186.6 2.9 copy.184
  189.6 1.6 copy.185
  191.2 1.6 copy.186
  193.8 2.1 copy-done
  197.3 2.5 copy.187
  199.9 4.8 %bitcast_add_fusion.2 = f32[1,32,64,128]{2,1,3,0:T(8,128)} fusion(f32[64,32,128]{0,1,2:T(8,128)S(1)} %copy-done.1, f32[64,128]{0,1:T(8,128)S(1)} %fusion.98, f32[64,128]{0,1:T(8,128)S(1)} %get-tuple-element.317, f32[128,64,64]{2,1,0:T(8,128)} %copy-done, bf16[1,32,64,128]{2,1,3,0:T(8,128)(2,1)} %copy.187), kind=kOutput, calls=%fused_computation.10.clone.1 | convolution fusion | flops 35913728 | bytes 4784128 | tf_op jit(solution)/shard_map/while/body/eval_jaxpr/nhgw,ndgw->ndhw/dot_general | solution.py:36
  204.7 3.0 copy.188
  210.9 3.7 %fusion.95 = (f32[64,128]{1,0:T(8,128)S(1)}, f32[64,128,128]{1,2,0:T(8,128)S(1)}) fusion(f32[64,128,128]{1,2,0:T(8,128)S(1)} %fusion.94), kind=kOutput, calls=%fused_computation.94.clone.1 | output fusion | flops 4194431 | bytes 8421376 | tf_op jit(solution)/shard_map/while/body/eval_jaxpr/sub | solution.py:19
  216.4 2.9 copy.184
  219.4 1.6 copy.185
  221.0 1.6 copy.186
  223.7 2.1 copy-done
  227.2 2.5 copy.187
  229.7 4.8 %bitcast_add_fusion.2 = f32[1,32,64,128]{2,1,3,0:T(8,128)} fusion(f32[64,32,128]{0,1,2:T(8,128)S(1)} %copy-done.1, f32[64,128]{0,1:T(8,128)S(1)} %fusion.98, f32[64,128]{0,1:T(8,128)S(1)} %get-tuple-element.317, f32[128,64,64]{2,1,0:T(8,128)} %copy-done, bf16[1,32,64,128]{2,1,3,0:T(8,128)(2,1)} %copy.187), kind=kOutput, calls=%fused_computation.10.clone.1 | convolution fusion | flops 35913728 | bytes 4784128 | tf_op jit(solution)/shard_map/while/body/eval_jaxpr/nhgw,ndgw->ndhw/dot_general | solution.py:36
  234.5 3.0 copy.188
  241.7 32.8 %all-reduce = (f32[128,16]{0,1:T(8,128)S(1)}, f32[128,16]{0,1:T(8,128)S(1)}) all-reduce(f32[128,16]{0,1:T(8,128)S(1)} %get-tuple-element.160, f32[128,16]{0,1:T(8,128)S(1)} %get-tuple-element.159), channel_id=1, replica_groups=mesh['st'=32,'ha'=8] {'ha'}, use_global_device_ids=true, to_apply=%region_26.27 | all-reduce | flops 4096 | bytes 32768 | tf_op jit(solution)/shard_map/psum | solution.py:171
  274.5 1.5 convert_bitcast_fusion
  276.2 3.6 fusion.57
  280.6 68.7 %all-reduce.4.cloned.1.call-done = (bf16[2,64,128]{2,1,0:T(8,128)(2,1)}, bf16[2,64,128]{2,1,0:T(8,128)(2,1)}) async-done(((bf16[2,64,128]{2,1,0:T(8,128)(2,1)}, bf16[2,64,128]{2,1,0:T(8,128)(2,1)}), (bf16[2,64,128]{2,1,0:T(8,128)(2,1)}, bf16[2,64,128]{2,1,0:T(8,128)(2,1)})) %all-reduce.4.cloned.1.call-update) | async-done | bytes 65552 | tf_op jit(solution)/shard_map/psum | solution.py:169
  (159 shorter events, 94.2 us)
Async XLA Ops:
  7.2 15.6 %copy-start.2 = (bf16[2,32,64,128]{3,2,1,0:T(8,128)(2,1)S(1)}, bf16[2,32,64,128]{3,2,1,0:T(8,128)(2,1)}, u32[]{:S(2)}) copy-start(bf16[2,32,64,128]{3,2,1,0:T(8,128)(2,1)} %param.21) | copy-start | bytes 3145732
  7.2 17.2 %copy-start.18 = (s32[4]{0:T(128)S(1)}, s32[4]{0:T(128)}, u32[]{:S(2)}) copy-start(s32[4]{0:T(128)} %param.16) | copy-start | bytes 52
  7.2 17.4 %copy-start.4 = (bf16[2,32,64,128]{3,2,1,0:T(8,128)(2,1)S(1)}, bf16[2,32,64,128]{3,2,1,0:T(8,128)(2,1)}, u32[]{:S(2)}) copy-start(bf16[2,32,64,128]{3,2,1,0:T(8,128)(2,1)} %param.20) | copy-start | bytes 3145732
  7.2 19.0 %copy-start.5 = (bf16[2,32,64,128]{3,2,1,0:T(8,128)(2,1)S(1)}, bf16[2,32,64,128]{3,2,1,0:T(8,128)(2,1)}, u32[]{:S(2)}) copy-start(bf16[2,32,64,128]{3,2,1,0:T(8,128)(2,1)} %param.19) | copy-start | bytes 3145732
  8.9 0.6 copy-start.13
  15.2 13.2 %all-to-all-start.4 = ((bf16[32,2,2048]{2,1,0:T(2,128)(2,1)}), bf16[32,2,2048]{2,1,0:T(2,128)(2,1)S(1)}, u32[]{:S(2)}, u32[]{:S(2)}) async-start(bf16[32,2,2048]{2,1,0:T(2,128)(2,1)} %reshape.291), calls=%async_computation.4 | async-start | bytes 524288 | tf_op jit(solution)/shard_map/all_to_all | solution.py:141
  28.4 21.6 %all-to-all-start.2 = ((bf16[2,32,64,128]{3,1,0,2:T(8,128)(2,1)}), bf16[2,32,64,128]{3,1,0,2:T(8,128)(2,1)}, u32[]{:S(2)}, u32[]{:S(2)}) async-start(bf16[2,32,64,128]{3,1,0,2:T(8,128)(2,1)} %copy.132), calls=%async_computation.2 | async-start | bytes 2097152 | tf_op jit(solution)/shard_map/all_to_all | solution.py:116
  50.1 41.3 %all-to-all-start = ((bf16[2,32,64,128]{3,1,0,2:T(8,128)(2,1)}), bf16[2,32,64,128]{3,1,0,2:T(8,128)(2,1)S(1)}, u32[]{:S(2)}, u32[]{:S(2)}) async-start(bf16[2,32,64,128]{3,1,0,2:T(8,128)(2,1)} %copy.124), calls=%async_computation | async-start | bytes 2097152 | tf_op jit(solution)/shard_map/all_to_all | solution.py:115
  57.4 41.5 %copy-start.10 = (bf16[1,32,8192]{2,1,0:T(8,128)(2,1)S(1)}, bf16[1,32,8192]{2,1,0:T(8,128)(2,1)}, u32[]{:S(2)}) copy-start(bf16[1,32,8192]{2,1,0:T(8,128)(2,1)} %reshape_squeeze.13) | copy-start | bytes 1572868
  58.8 1.4 copy-start.11
  63.0 1.4 copy-start.11
  67.3 1.4 copy-start.11
  71.5 1.4 copy-start.11
  75.7 1.4 copy-start.11
  79.9 1.4 copy-start.11
  84.1 1.4 copy-start.11
  88.4 1.4 copy-start.11
  91.4 7.5 %copy-start.6 = (bf16[2,32,64,128]{3,1,0,2:T(8,128)(2,1)}, bf16[2,32,64,128]{3,1,0,2:T(8,128)(2,1)S(1)}, u32[]{:S(2)}) copy-start(bf16[2,32,64,128]{3,1,0,2:T(8,128)(2,1)S(1)} %all-to-all-done) | copy-start | bytes 3145732
  91.4 53.4 %all-to-all-start.1 = ((bf16[2,32,64,128]{3,1,0,2:T(8,128)(2,1)}), bf16[2,32,64,128]{3,1,0,2:T(8,128)(2,1)}, u32[]{:S(2)}, u32[]{:S(2)}) async-start(bf16[2,32,64,128]{3,1,0,2:T(8,128)(2,1)} %copy.127), calls=%async_computation.1 | async-start | bytes 2097152 | tf_op jit(solution)/shard_map/all_to_all | solution.py:114
  133.6 7.7 %copy-start.7 = (bf16[2,32,64,128]{3,1,0,2:T(8,128)(2,1)S(1)}, bf16[2,32,64,128]{3,1,0,2:T(8,128)(2,1)}, u32[]{:S(2)}) copy-start(bf16[2,32,64,128]{3,1,0,2:T(8,128)(2,1)} %copy-done.6) | copy-start | bytes 3145732
  141.4 16.9 %copy-start.12 = (pred[64,64]{0,1:T(8,128)(4,1)S(1)}, pred[64,64]{0,1:T(8,128)(4,1)}, u32[]{:S(2)}) copy-start(pred[64,64]{0,1:T(8,128)(4,1)} %broadcast_compare_fusion) | copy-start | bytes 12292
  144.9 26.1 %all-to-all-start.5 = ((bf16[32,2,2048]{2,1,0:T(2,128)(2,1)}), bf16[32,2,2048]{2,1,0:T(2,128)(2,1)S(1)}, u32[]{:S(2)}, u32[]{:S(2)}) async-start(bf16[32,2,2048]{2,1,0:T(2,128)(2,1)} %reshape.293), calls=%async_computation.5 | async-start | bytes 524288 | tf_op jit(solution)/shard_map/all_to_all | solution.py:155
  161.9 3.0 copy-start.8
  171.0 103.5 %all-to-all-start.3 = ((bf16[64,32,2,128]{3,1,2,0:T(8,128)(2,1)}), bf16[64,32,2,128]{3,1,2,0:T(8,128)(2,1)}, u32[]{:S(2)}, u32[]{:S(2)}) async-start(bf16[64,32,2,128]{3,1,2,0:T(8,128)(2,1)} %copy.137), calls=%async_computation.3 | async-start | bytes 2097152 | tf_op jit(solution)/shard_map/all_to_all | solution.py:119
  178.4 170.9 %all-reduce.4.cloned.1.call-start = ((), (), s32[]{:S(2)}) async-start(), calls=%async_computation.6 | async-start | bytes 131072 | tf_op jit(solution)/shard_map/psum | solution.py:169
  178.9 59.9 %copy-start.16 = (s32[128]{0:T(128)S(1)}, s32[128]{0:T(128)}, u32[]{:S(2)}) copy-start(s32[128]{0:T(128)} %param.18) | copy-start | bytes 1540
  178.9 61.6 %copy-start.14 = (s32[128]{0:T(128)S(1)}, s32[128]{0:T(128)}, u32[]{:S(2)}) copy-start(s32[128]{0:T(128)} %copy-done.13) | copy-start | bytes 1540
  192.8 4.5 %copy-start.3 = (bf16[2,32,64,128]{3,2,1,0:T(8,128)(2,1)S(1)}, bf16[2,32,64,128]{3,2,1,0:T(8,128)(2,1)}, u32[]{:S(2)}) copy-start(bf16[2,32,64,128]{3,2,1,0:T(8,128)(2,1)} %get-tuple-element.346) | copy-start | bytes 3145732 | tf_op jit(solution)/shard_map/while
  193.8 2.1 copy-start
  193.8 6.0 %copy-start.1 = (f32[64,32,128]{0,1,2:T(8,128)S(1)}, f32[64,32,128]{0,1,2:T(8,128)}, u32[]{:S(2)}) copy-start(f32[64,32,128]{0,1,2:T(8,128)} %copy.184) | copy-start | bytes 3145732 | tf_op jit(solution)/shard_map/while
  222.7 4.5 %copy-start.3 = (bf16[2,32,64,128]{3,2,1,0:T(8,128)(2,1)S(1)}, bf16[2,32,64,128]{3,2,1,0:T(8,128)(2,1)}, u32[]{:S(2)}) copy-start(bf16[2,32,64,128]{3,2,1,0:T(8,128)(2,1)} %get-tuple-element.346) | copy-start | bytes 3145732 | tf_op jit(solution)/shard_map/while
  223.7 2.1 copy-start
  223.7 6.0 %copy-start.1 = (f32[64,32,128]{0,1,2:T(8,128)S(1)}, f32[64,32,128]{0,1,2:T(8,128)}, u32[]{:S(2)}) copy-start(f32[64,32,128]{0,1,2:T(8,128)} %copy.184) | copy-start | bytes 3145732 | tf_op jit(solution)/shard_map/while
  240.3 35.9 %copy-start.9 = (bf16[2,32,64,128]{3,2,1,0:T(8,128)(2,1)S(1)}, bf16[2,32,64,128]{3,2,1,0:T(8,128)(2,1)}, u32[]{:S(2)}) copy-start(bf16[2,32,64,128]{3,2,1,0:T(8,128)(2,1)} %param.22) | copy-start | bytes 3145732
  276.2 3.6 %copy-start.15 = (f32[32]{0:T(128)S(1)}, f32[32]{0:T(128)}, u32[]{:S(2)}) copy-start(f32[32]{0:T(128)} %param.25) | copy-start | bytes 388
  276.2 73.9 %copy-start.17 = (f32[32]{0:T(128)S(1)}, f32[32]{0:T(128)}, u32[]{:S(2)}) copy-start(f32[32]{0:T(128)} %param.23) | copy-start | bytes 388
Sparse Core Ops, SparseCore 0:
  280.0 69.2 all-reduce.3
where the time goes:
time: 366 us; the launch traced here: 359 us
  waiting for transfers between devices  78.7 us (22%)
  local copies, waits for them, and re-layouts  73.2 us (20%)
  matrix products  68.8 us (19%)
  starting transfers between devices  45.7 us (12%)
  other arithmetic  44.7 us (12%)
  blocking collectives  32.8 us (9%)
  between operations  14.7 us (4%)
    psum x1, waiting for transfers between devices, per_device(): lax.psum(pixel_squares.astype(jnp.bfloat16), 'ha').astype(jnp.float32)  68.7 us
    psum x1, blocking collectives, per_device(): inst_totals, inst_squares = lax.psum((inst_totals, inst_squares), 'ha')  32.8 us
    reduce_sum x19, other arithmetic, soft_weights(): jnp.sum(raised, axis=axis_num, keepdims=True)  27.3 us
    dot_general x16, matrix products, attend_block(): jnp.einsum('nrt,ndt->rnd', weights, value_h, preferred_element_type=jnp.f...  23.8 us
    dot_general x16, matrix products, attend_block(): jnp.einsum('rnd,ndt->nrt', query_block, key_h, preferred_element_type=jnp...  21.9 us
    another operation x7, local copies, waits for them, and re-layouts  14.3 us
    dynamic_slice x10, local copies, waits for them, and re-layouts, per_device(): spatial = lax.map(spatial_frame, (pix_q, pix_k, pix_v))  14.1 us
    unnamed x38, local copies, waits for them, and re-layouts  12.8 us
  transfers between devices with their start and end apart: 7, of which 3 were waited for; matrix products, arithmetic and copies ran while one was open for 46% of the time, Pallas kernels for 0%

commit v1 on v0

v1 whole, which is shorter than its diff:
```python
import jax
import jax.numpy as jnp
from jax import lax
from jax.experimental import pallas as pl
from jax.experimental.pallas import tpu as pltpu
from jax.sharding import PartitionSpec as P

F32 = jnp.float32
BF = jnp.bfloat16
MESH = pl.DeviceIdType.MESH
C = 256
HD = 32
EPSILON = 1e-05
MASKED = -1e30
SCALE2 = (HD**-0.5) * 1.4426950408889634
DEAD = 16384.0
CHUNK = 2048
BIG, SMALL = 512, 128
QROWS = 2048 + BIG
VM = pl.BlockSpec(memory_space=pltpu.VMEM)
SM = pl.BlockSpec(memory_space=pltpu.SMEM)


def rows_at(start, size):
    return pl.ds(pl.multiple_of(start, size), size)


def scores_of(k, q):
    return lax.dot_general(k, q, (((0,), (0,)), ((), ())), preferred_element_type=F32)


def width_step(q, k, v):
    s = scores_of(k, q) * SCALE2
    e = jnp.exp2(s - jnp.max(s, axis=0, keepdims=True))
    total = jnp.sum(e, axis=0, keepdims=True)
    return jnp.dot(v, e.astype(BF), preferred_element_type=F32) * (1.0 / total)


def pair_step(q, k, v, low, mask):
    s = scores_of(k, q)
    s = jnp.where(low, s[:64], s[64:]) * SCALE2
    if mask is not None:
        s = s + mask
    e = jnp.exp2(s - jnp.max(s, axis=0, keepdims=True))
    total = jnp.sum(e, axis=0, keepdims=True)
    zero = jnp.zeros_like(e)
    p = jnp.concatenate([jnp.where(low, e, zero), jnp.where(low, zero, e)], axis=0)
    return jnp.dot(v, p.astype(BF), preferred_element_type=F32) * (1.0 / total)


def attend_pairs(qs, ks, vs, os, mask, count, unroll):
    low = lax.broadcasted_iota(jnp.int32, (64, 128), 1) < 64

    def body(b, _):
        r = rows_at(b * 32, 32)
        os[r, :] = pair_step(
            qs[r, :].astype(BF), ks[r, :].astype(BF), vs[r, :].astype(BF), low, mask
        )
        return 0

    lax.fori_loop(0, count, body, 0, unroll=unroll)


def width_all(buf, acc, unroll):
    for f in range(2):

        def body(d, _):
            for half in range(2):
                lanes = pl.ds(half * 128, 128)
                o = width_step(
                    buf[d, pl.ds(f * 32, 32), lanes],
                    buf[d, pl.ds(64 + f * 32, 32), lanes],
                    buf[d, pl.ds(128 + f * 32, 32), lanes],
                )
                acc[pl.ds(f * 2048 + d * 2 + half, 32, stride=64), :] = o
            return 0

        lax.fori_loop(0, 32, body, 0, unroll=unroll)


def height_in(src, dst):
    def body(c, _):
        t = jnp.concatenate([src[0, c], src[1, c]], axis=0).astype(F32)
        dst[pl.ds(c, 128, stride=32), :] = t.T
        return 0

    lax.fori_loop(0, 32, body, 0, unroll=4)


def height_out(os, features, wide, acc):
    def body(c, _):
        t = os[pl.ds(c, 128, stride=32), :].T
        for f in range(2):
            r = rows_at(f * 2048 + c * 64, 64)
            acc[r, :] = wide[r, :] + t[f * 64 : (f + 1) * 64] + features[f, c].astype(F32)
        return 0

    lax.fori_loop(0, 32, body, 0, unroll=4)


BASE = (
    (1, 0), (0, 1), (3, 0), (0, 3), (2, 0), (0, 2), (1, 1), (3, 3),
    (1, 3), (3, 1), (2, 1), (1, 2), (2, 3), (3, 2), (2, 2),
)
MOVES = tuple((a, b, c) for a, b in BASE for c in (0, 1)) + ((0, 0, 1),)


def peer_to(me, move):
    dx, dy, dc = move
    x, y, core = me // 8, (me // 2) % 4, me % 2
    sx = dx + core * ((4 - 2 * dx) % 4)
    sy = dy + core * ((4 - 2 * dy) % 4)
    return ((x + sx) % 4) * 8 + ((y + sy) % 4) * 2 + (core + dc) % 2


def hello(axis, size):
    me = lax.axis_index(axis)
    barrier = pltpu.get_barrier_semaphore()

    def signal(s, _):
        pl.semaphore_signal(
            barrier, inc=1, device_id={axis: lax.rem(me + s, size)}, device_id_type=MESH
        )
        return 0

    lax.fori_loop(1, size, signal, 0)


def greeted(total):
    pl.semaphore_wait(pltpu.get_barrier_semaphore(), total)


def columns_of(row):
    return jnp.broadcast_to(row, (128, 128)).T


def slots_of(trow):
    target = trow.astype(F32)
    one = lax.broadcasted_iota(jnp.int32, (128, 128), 0)
    two = lax.broadcasted_iota(jnp.int32, (128, 128), 1)
    before = jnp.where((columns_of(target) == target) & (one < two), 1.0, 0.0)
    arrival = jnp.sum(before, axis=0, keepdims=True)
    frame = lax.broadcasted_iota(jnp.int32, (64, 128), 0)
    return arrival, jnp.where(frame == trow, 1.0, 0.0).astype(BF)


def first_kernel(
    q, k, v, inst, trow, qrow, buf, kflat, got, stage, rows, msg, raw,
    send_sem, recv_sem, own_sem, load_sem,
):
    me = lax.axis_index("st")
    loads = []
    for number, src in enumerate((k, v, q)):
        load = pltpu.make_async_copy(src, raw.at[number], load_sem.at[number])
        load.start()
        loads.append(load)
    hello("st", 32)
    arrival, place = slots_of(trow[...])
    live = qrow[...].astype(F32)
    group = lax.broadcasted_iota(jnp.int32, (128, 128), 0) // 32
    here = group.astype(F32) == arrival
    counts = lax.dot_general(
        place,
        jnp.where(here, live, 0.0).astype(BF),
        (((1,), (1,)), ((), ())),
        preferred_element_type=F32,
    )
    for r in range(16):
        x = inst[r].astype(F32)
        y = jnp.where(here, jnp.concatenate([x, x, x, x], axis=0), 0.0).astype(BF)
        put = lax.dot_general(
            place, y, (((1,), (1,)), ((), ())), preferred_element_type=F32
        )
        rows[pl.ds(r, 64, stride=16), :] = jnp.where(counts > r + 0.5, put, DEAD)
    msg[...] = rows[...].astype(BF)
    greeted(31)
    copies = []
    for i, move in enumerate(MOVES):
        peer = peer_to(me, move)
        copy = pltpu.make_async_remote_copy(
            src_ref=msg.at[rows_at(peer * 32, 32)],
            dst_ref=got.at[rows_at(me * 32, 32)],
            send_sem=send_sem.at[i],
            recv_sem=recv_sem.at[i],
            device_id={"st": peer},
            device_id_type=MESH,
        )
        copy.start()
        copies.append(copy)
    own = pltpu.make_async_copy(
        msg.at[rows_at(me * 32, 32)], got.at[rows_at(me * 32, 32)], own_sem
    )
    own.start()
    for number in range(3):
        base = (64, 128, 0)[number]
        loads[number].wait()

        def widen(c, _):
            for f in range(2):
                stage[rows_at(f * 2048 + c * 64, 64), :] = raw[number, f, c].astype(F32)
            return 0

        lax.fori_loop(0, 32, widen, 0, unroll=4)

        def body(d, _):
            for half in range(2):
                x = stage[pl.ds(d * 2 + half, 64, stride=64), :].astype(BF)
                buf[d, pl.ds(base, 64), pl.ds(half * 128, 128)] = x
                if number == 0:
                    kflat[:, rows_at((d * 2 + half) * 128, 128)] = x
            return 0

        lax.fori_loop(0, 32, body, 0, unroll=4)
    own.wait()
    for copy in copies:
        copy.wait()


def first(q, k, v, inst, trow, qrow):
    sd = jax.ShapeDtypeStruct
    dma = pltpu.SemaphoreType.DMA
    any_space = pl.BlockSpec(memory_space=pl.ANY)
    return pl.pallas_call(
        first_kernel,
        out_shape=(sd((32, 192, 256), BF), sd((64, 8192), BF), sd((1024, 128), BF)),
        in_specs=[any_space] * 3 + [VM] * 3,
        out_specs=(VM, VM, VM),
        scratch_shapes=[
            pltpu.VMEM((4096, 128), F32),
            pltpu.VMEM((1024, 128), F32),
            pltpu.VMEM((1024, 128), BF),
            pltpu.VMEM((3, 2, 32, 64, 128), BF),
            dma((31,)),
            dma((31,)),
            dma,
            dma((3,)),
        ],
        compiler_params=pltpu.CompilerParams(
            collective_id=0, has_side_effects=True, vmem_limit_bytes=20 << 20
        ),
        cost_estimate=pl.CostEstimate(flops=1 << 24, bytes_accessed=8 << 20, transcendentals=0),
    )(q, k, v, inst, trow, qrow)


def cross_block(q, kflat, values, f):
    most, acc = None, None
    for j in range(8192 // CHUNK):
        s = jnp.dot(
            q,
            kflat[f * 32 : (f + 1) * 32, j * CHUNK : (j + 1) * CHUNK],
            preferred_element_type=F32,
        )
        here = jnp.max(s, axis=1, keepdims=True) * SCALE2
        new = here if most is None else jnp.maximum(most, here)
        p = jnp.exp2(s * SCALE2 - new).astype(BF)
        o = jnp.dot(p, values[f, pl.ds(j * CHUNK, CHUNK), :], preferred_element_type=F32)
        acc = o if acc is None else acc * jnp.exp2(most - new) + o
        most = new
    return acc / acc[:, 32:33]


def cross_kernel(got, kflat, buf, ans, acc, values, wide, packed, solved, live, counts, starts, sem):
    wide[...] = got[...].astype(F32)
    alive = jnp.where(wide[...] < DEAD / 2, 1.0, 0.0).reshape(64, 16, 128)
    live[...] = jnp.sum(alive, axis=1).astype(jnp.int32)
    down = pltpu.make_async_copy(live, counts, sem)
    down.start()

    def turn(d, _):
        for f in range(2):
            t = buf[d, pl.ds(128 + f * 32, 32), :].astype(F32)
            one = jnp.ones((32, 256), F32)
            full = jnp.concatenate([t, one, one, one], axis=0)
            values[f, rows_at(d * 256, 256), :] = full.T.astype(BF)
        return 0

    lax.fori_loop(0, 32, turn, 0, unroll=2)
    down.wait()
    width_all(buf, acc, 8)

    for f in range(2):

        def pack(src, offset):
            block = wide[pl.ds(pl.multiple_of(src * 32 + f * 16, 16), 16), :]
            for j in range(4):
                starts[src * 2 + f, j] = offset
                moved = block if j == 0 else pltpu.roll(block, 128 - 32 * j, 1)
                packed[pl.ds(offset, 16), :] = moved
                offset = offset + counts[src * 2 + f, 32 * j]
            return offset

        total = lax.fori_loop(0, 32, pack, 0)
        many = (total + SMALL - 1) // BIG
        rest = jnp.maximum(total - many * BIG, 0)

        def big(b, _):
            r = rows_at(b * BIG, BIG)
            solved[r, :] = cross_block(packed[r, :][:, :32].astype(BF), kflat, values, f)
            return 0

        lax.fori_loop(0, many, big, 0)

        def small(b, _):
            r = rows_at(many * BIG + b * SMALL, SMALL)
            solved[r, :] = cross_block(packed[r, :][:, :32].astype(BF), kflat, values, f)
            return 0

        lax.fori_loop(0, (rest + SMALL - 1) // SMALL, small, 0)
        row = lax.broadcasted_iota(jnp.int32, (16, 128), 0)
        group = lax.broadcasted_iota(jnp.int32, (16, 128), 1) // 32

        def unpack(src, _):
            out = jnp.zeros((16, 128), F32)
            for j in range(4):
                x = solved[pl.ds(starts[src * 2 + f, j], 16), :]
                moved = x if j == 0 else pltpu.roll(x, 32 * j, 1)
                keep = (group == j) & (row < counts[src * 2 + f, 32 * j])
                out = jnp.where(keep, moved, out)
            ans[pl.ds(pl.multiple_of(src * 32 + f * 16, 16), 16), :] = out.astype(BF)
            return 0

        lax.fori_loop(0, 32, unpack, 0)


def cross(got, kflat, buf):
    return pl.pallas_call(
        cross_kernel,
        out_shape=(
            jax.ShapeDtypeStruct((1024, 128), BF),
            jax.ShapeDtypeStruct((4096, 128), F32),
        ),
        in_specs=[VM] * 3,
        out_specs=(VM, VM),
        scratch_shapes=[
            pltpu.VMEM((2, 8192, 128), BF),
            pltpu.VMEM((1024, 128), F32),
            pltpu.VMEM((QROWS, 128), F32),
            pltpu.VMEM((QROWS, 128), F32),
            pltpu.VMEM((64, 128), jnp.int32),
            pltpu.SMEM((64, 128), jnp.int32),
            pltpu.SMEM((64, 4), jnp.int32),
            pltpu.SemaphoreType.DMA,
        ],
        compiler_params=pltpu.CompilerParams(vmem_limit_bytes=32 << 20),
        cost_estimate=pl.CostEstimate(
            flops=17 << 30, bytes_accessed=8 << 20, transcendentals=1 << 24
        ),
    )(got, kflat, buf)


def time_half(patch, mask, half, stage, qs, ks, vs, os, out):
    low = lax.broadcasted_iota(jnp.int32, (64, 128), 1) < 64
    lanes = pl.ds(half * 128, 128)
    for base, dst in ((0, qs), (64, ks), (128, vs)):

        def spread(i, _):
            stage[rows_at(i * 64, 64), :] = patch[i, pl.ds(base, 64), lanes].astype(F32)
            return 0

        lax.fori_loop(0, 32, spread, 0, unroll=4)

        def turn(b, _):
            one, two = pl.ds(b * 2, 64, stride=32), pl.ds(b * 2 + 1, 64, stride=32)
            t = jnp.concatenate([stage[one, :], stage[two, :]], axis=0).T
            top, end = t[:64], t[64:]
            dst[one, :] = jnp.where(low, top, pltpu.roll(end, 64, 1))
            dst[two, :] = jnp.where(low, pltpu.roll(top, 64, 1), end)
            return 0

        lax.fori_loop(0, 16, turn, 0, unroll=4)
    attend_pairs(qs, ks, vs, os, mask, 64, 16)

    def turn_back(b, _):
        one, two = pl.ds(b * 2, 64, stride=32), pl.ds(b * 2 + 1, 64, stride=32)
        x, y = os[one, :], os[two, :]
        top = jnp.where(low, x, pltpu.roll(y, 64, 1))
        end = jnp.where(low, pltpu.roll(x, 64, 1), y)
        t = jnp.concatenate([top, end], axis=0).T
        stage[one, :] = t[:64]
        stage[two, :] = t[64:]
        return 0

    lax.fori_loop(0, 16, turn_back, 0, unroll=4)

    def gather(i, _):
        out[half, i] = stage[rows_at(i * 64, 64), :].astype(BF)
        return 0

    lax.fori_loop(0, 32, gather, 0, unroll=4)


def last_kernel(
    patch, mask, ans, q, k, v, features, wide, inst, trow,
    acc, pall, irow, istat,
    raw, timed, tback, aback, stage, qs, ks, vs, os, arow, part, partbf, pgot, pnew,
    ipart, igot, tsend, trecv, asend, arecv, own_sem, zsend, zrecv, load_sem,
):
    me = lax.axis_index("st")
    mz = lax.axis_index("ha")
    hello("st", 32)
    hello("ha", 8)
    loads = []
    for number, src in enumerate((q, k, v, features)):
        load = pltpu.make_async_copy(src, raw.at[number], load_sem.at[number])
        load.start()
        loads.append(load)

    def to_st(src, dst, send, recv, i, peer):
        copy = pltpu.make_async_remote_copy(
            src_ref=src,
            dst_ref=dst,
            send_sem=send.at[i],
            recv_sem=recv.at[i],
            device_id={"st": peer},
            device_id_type=MESH,
        )
        copy.start()
        return copy

    def return_half(half):
        copies = [
            to_st(
                timed.at[half, peer_to(me, move)], tback.at[half, me],
                tsend.at[half], trecv.at[half], i, peer_to(me, move),
            )
            for i, move in enumerate(MOVES)
        ]
        own = pltpu.make_async_copy(
            timed.at[half, me], tback.at[half, me], own_sem.at[half]
        )
        own.start()
        return copies + [own]

    known = mask[...]
    time_half(patch, known, 0, stage, qs, ks, vs, os, timed)
    greeted(38)
    answers = []
    for i, move in enumerate(MOVES):
        peer = peer_to(me, move)
        answers.append(
            to_st(
                ans.at[rows_at(peer * 32, 32)], aback.at[rows_at(me * 32, 32)],
                asend, arecv, i, peer,
            )
        )
    own = pltpu.make_async_copy(
        ans.at[rows_at(me * 32, 32)], aback.at[rows_at(me * 32, 32)], own_sem.at[2]
    )
    own.start()
    answers.append(own)
    backs = return_half(0)
    time_half(patch, known, 1, stage, qs, ks, vs, os, timed)
    backs = backs + return_half(1)

    for load in loads:
        load.wait()
    height_in(raw.at[0], qs)
    height_in(raw.at[1], ks)
    height_in(raw.at[2], vs)
    attend_pairs(qs, ks, vs, os, None, 128, 16)
    height_out(os, raw.at[3], wide, acc)

    def exchange(src, dst, at_src, at_dst, which):
        copies = []
        for s in range(1, 8):
            peer = lax.rem(mz + s, 8)
            copy = pltpu.make_async_remote_copy(
                src_ref=at_src(src, peer),
                dst_ref=at_dst(dst),
                send_sem=zsend.at[which, s],
                recv_sem=zrecv.at[which, s],
                device_id={"ha": peer},
                device_id_type=MESH,
            )
            copy.start()
            copies.append(copy)
        return copies

    arrival, place = slots_of(trow[...])
    for copy in answers:
        copy.wait()
    arow[...] = aback[...].astype(F32)
    for r in range(16):
        mine = lax.dot_general(
            arow[pl.ds(r, 64, stride=16), :].astype(BF),
            place,
            (((0,), (0,)), ((), ())),
            preferred_element_type=F32,
        )
        pre = inst[r].astype(F32)
        for j in range(4):
            pre = pre + jnp.where(arrival == j, mine[j * 32 : (j + 1) * 32], 0.0)
        irow[r] = pre
        ipart[pl.ds(r, 1), :] = jnp.sum(pre, axis=0, keepdims=True)
        ipart[pl.ds(16 + r, 1), :] = jnp.sum(pre * pre, axis=0, keepdims=True)
    shared = exchange(ipart, igot, lambda a, p: a, lambda a: a.at[mz], 0)
    igot[mz] = ipart[...]

    for copy in backs:
        copy.wait()

    def add_time(d, _):
        for half in range(2):
            r = pl.ds(d * 2 + half, 64, stride=64)
            acc[r, :] = acc[r, :] + tback[half, d].astype(F32)
        return 0

    lax.fori_loop(0, 32, add_time, 0, unroll=4)
    for f in range(2):

        def sums(c, carry):
            x = acc[rows_at(f * 2048 + c * 64, 64), :]
            return carry[0] + x, carry[1] + x * x

        zero = jnp.zeros((64, 128), F32)
        tot, sqr = lax.fori_loop(0, 32, sums, (zero, zero), unroll=4)
        for b in range(4):
            part[f * 4 + b, 0:16, :] = tot[b * 16 : (b + 1) * 16]
            part[f * 4 + b, 16:32, :] = sqr[b * 16 : (b + 1) * 16]
    partbf[...] = part[...].astype(BF)
    scattered = exchange(partbf, pgot, lambda a, p: a.at[p], lambda a: a.at[mz], 1)
    pgot[mz] = partbf[mz]
    for copy in shared:
        copy.wait()
    total = igot[0]
    for z in range(1, 8):
        total = total + igot[z]
    mean = total[:16] / C
    istat[0:16, :] = mean
    istat[16:32, :] = lax.rsqrt(total[16:] / C - mean * mean + EPSILON)
    for copy in scattered:
        copy.wait()
    total = pgot[0].astype(F32)
    for z in range(1, 8):
        total = total + pgot[z].astype(F32)
    mean = total[:16] / C
    pnew[0:16, :] = mean
    pnew[16:32, :] = lax.rsqrt(total[16:] / C - mean * mean + EPSILON)
    gathered = exchange(pnew, pall, lambda a, p: a, lambda a: a.at[mz], 2)
    pall[mz] = pnew[...]
    for copy in gathered:
        copy.wait()


def last(patch, mask, ans, q, k, v, features, wide, inst, trow):
    sd = jax.ShapeDtypeStruct
    dma = pltpu.SemaphoreType.DMA
    any_space = pl.BlockSpec(memory_space=pl.ANY)
    return pl.pallas_call(
        last_kernel,
        out_shape=(
            sd((4096, 128), F32),
            sd((8, 32, 128), F32),
            sd((16, 32, 128), F32),
            sd((32, 128), F32),
        ),
        in_specs=[VM] * 3 + [any_space] * 4 + [VM] * 3,
        out_specs=(VM, VM, VM, VM),
        scratch_shapes=[
            pltpu.VMEM((4, 2, 32, 64, 128), BF),
            pltpu.VMEM((2, 32, 64, 128), BF),
            pltpu.VMEM((2, 32, 64, 128), BF),
            pltpu.VMEM((1024, 128), BF),
            pltpu.VMEM((2048, 128), F32),
            pltpu.VMEM((4096, 128), F32),
            pltpu.VMEM((4096, 128), F32),
            pltpu.VMEM((4096, 128), F32),
            pltpu.VMEM((4096, 128), F32),
            pltpu.VMEM((1024, 128), F32),
            pltpu.VMEM((8, 32, 128), F32),
            pltpu.VMEM((8, 32, 128), BF),
            pltpu.VMEM((8, 32, 128), BF),
            pltpu.VMEM((32, 128), F32),
            pltpu.VMEM((32, 128), F32),
            pltpu.VMEM((8, 32, 128), F32),
            dma((2, 31)),
            dma((2, 31)),
            dma((31,)),
            dma((31,)),
            dma((3,)),
            dma((3, 8)),
            dma((3, 8)),
            dma((4,)),
        ],
        compiler_params=pltpu.CompilerParams(
            collective_id=1, has_side_effects=True, vmem_limit_bytes=34 << 20
        ),
        cost_estimate=pl.CostEstimate(
            flops=1 << 32, bytes_accessed=12 << 20, transcendentals=1 << 21
        ),
    )(patch, mask, ans, q, k, v, features, wide, inst, trow)


def norm_kernel(acc, pall, irow, istat, qrow, pgain, igain, pixel_out, inst_out):
    for f in range(2):

        def finish(c, _):
            r = rows_at(f * 2048 + c * 64, 64)
            gain = pgain[c]
            x = acc[r, :]
            for b in range(4):
                low = slice(b * 16, (b + 1) * 16)
                y = (x[low] - pall[f * 4 + b, 0:16, :]) * pall[f * 4 + b, 16:32, :] * gain
                pixel_out[f, c, low, :] = y.astype(BF)
            return 0

        lax.fori_loop(0, 32, finish, 0, unroll=4)
    row = igain[...]
    gains = columns_of(jnp.concatenate([row, row, row, row], axis=1))[:32]
    live = qrow[...]
    for r in range(16):
        y = (irow[r] - istat[pl.ds(r, 1), :]) * istat[pl.ds(16 + r, 1), :] * gains
        inst_out[r] = jnp.where(live > r, y, 0.0).astype(BF)


def norm(acc, pall, irow, istat, qrow, pgain, igain):
    sd = jax.ShapeDtypeStruct
    return pl.pallas_call(
        norm_kernel,
        out_shape=(sd((2, 32, 64, 128), BF), sd((16, 32, 128), BF)),
        in_specs=[VM] * 5 + [SM, VM],
        out_specs=(VM, VM),
        compiler_params=pltpu.CompilerParams(vmem_limit_bytes=12 << 20),
        cost_estimate=pl.CostEstimate(flops=1 << 22, bytes_accessed=3 << 20, transcendentals=0),
    )(acc, pall, irow, istat, qrow, pgain, igain)


def per_device(
    clip_lengths,
    inst_frame,
    query_rows,
    pix_q,
    pix_k,
    pix_v,
    features,
    pixel_gain,
    inst_query,
    inst_gain,
):
    clip_ends = jnp.cumsum(clip_lengths)
    frame_ids = jnp.arange(64, dtype=jnp.int32)
    clip_of = jnp.sum((clip_ends[None, :] <= frame_ids[:, None]).astype(jnp.int32), axis=1)
    same_clip = clip_of[:, None] == clip_of[None, :]
    mask = jnp.where(same_clip, 0.0, MASKED).astype(F32)
    mask = jnp.concatenate([mask, mask], axis=1)
    trow = inst_frame.reshape(1, 128)
    qrow = query_rows.reshape(1, 128)
    inst = inst_query.transpose(1, 2, 0)
    buf, kflat, got = first(pix_q, pix_k, pix_v, inst, trow, qrow)
    buf, got = lax.optimization_barrier((buf, got))
    patch = lax.all_to_all(buf, "st", split_axis=0, concat_axis=0, tiled=True)
    ans, wide = cross(got, kflat, buf)
    acc, pall, irow, istat = last(
        patch, mask, ans, pix_q, pix_k, pix_v, features, wide, inst, trow
    )
    pixel_out, inst_out = norm(
        acc, pall, irow, istat, qrow, pixel_gain, inst_gain.reshape(1, 32)
    )
    return pixel_out, inst_out.transpose(2, 0, 1)


def solution(mesh):
    placed = (
        P(),
        P("st", None),
        P("st"),
        P("st", "ha", None, None),
        P("st", "ha", None, None),
        P("st", "ha", None, None),
        P("st", "ha", None, None),
        P("ha"),
        P("st", None, "ha"),
        P("ha"),
    )
    return jax.shard_map(
        per_device,
        mesh=mesh,
        in_specs=placed,
        out_specs=(P("st", "ha", None, None), P("st", None, "ha")),
        check_vma=False,
    )
```

time: 366 us -> 135 us (0.37); the launches traced: 359 us -> 135 us
  Pallas kernels: 0 us -> 103 us
  waiting for transfers between devices: 78.7 us -> 0.01 us
  matrix products: 68.8 us -> 0 us
  local copies, waits for them, and re-layouts: 73.2 us -> 22.8 us
  other arithmetic: 44.7 us -> 0.42 us
  starting transfers between devices: 45.7 us -> 7.52 us
  blocking collectives: 32.8 us -> 0 us
  between operations: 14.7 us -> 0.75 us
    pallas_call x0 -> x4, Pallas kernels: none -> 103 us  [the longest x1 52.6 us: last(): pl.pallas_call(last_kernel, out_shape=(sd((4096, 128), F32), sd((8, 32, 1...]
    dot_general x44 -> x0, matrix products: 68.8 us -> none  [the longest x16 23.8 us: attend_block(): jnp.einsum('nrt,ndt->rnd', weights, value_h, preferred_element_type=jnp.f...]
    psum x1 -> x0, waiting for transfers between devices: 68.7 us -> none  [per_device(): lax.psum(pixel_squares.astype(jnp.bfloat16), 'ha').astype(jnp.float32)]
    all_to_all x6 -> x1, starting transfers between devices: 45.3 us -> 7.52 us  [per_device(): patch = lax.all_to_all(buf, 'st', split_axis=0, concat_axis=0, tiled=True)]
    psum x1 -> x0, blocking collectives: 32.8 us -> none  [per_device(): inst_totals, inst_squares = lax.psum((inst_totals, inst_squares), 'ha')]
    reduce_sum x21 -> x0, other arithmetic: 31.8 us -> none  [the longest x19 27.3 us: soft_weights(): jnp.sum(raised, axis=axis_num, keepdims=True)]
    another operation x12 -> x0, local copies, waits for them, and re-layouts: 17.1 us -> none
    dynamic_slice x10 -> x0, local copies, waits for them, and re-layouts: 14.1 us -> none  [per_device(): spatial = lax.map(spatial_frame, (pix_q, pix_k, pix_v))]
  transfers between devices with their start and end apart: 7 -> 1, of which waited for: 3 -> 0; matrix products, arithmetic and copies ran while one was open for 46% -> 0% of each run, Pallas kernels for 0% -> 28%
where the time goes in v1:
time: 135 us
  Pallas kernels  103 us (76%)
  local copies, waits for them, and re-layouts  22.8 us (17%)
  starting transfers between devices  7.52 us (6%)
    pallas_call x1, Pallas kernels, last(): pl.pallas_call(last_kernel, out_shape=(sd((4096, 128), F32), sd((8, 32, 1...  52.6 us
    pallas_call x1, Pallas kernels, cross(): pl.pallas_call(cross_kernel, out_shape=(jax.ShapeDtypeStruct((1024, 128),...  37.9 us
    unnamed x52, local copies, waits for them, and re-layouts  22.8 us
    pallas_call x1, Pallas kernels, first(): pl.pallas_call(first_kernel, out_shape=(sd((32, 192, 256), BF), sd((64, 8...  10.8 us
    all_to_all x1, starting transfers between devices, per_device(): patch = lax.all_to_all(buf, 'st', split_axis=0, concat_axis=0, tiled=True)  7.52 us
  transfers between devices with their start and end apart: 1, of which 0 were waited for; matrix products, arithmetic and copies ran while one was open for 0% of the time, Pallas kernels for 28%

profile of v1, /device:TPU:14, one launch (start us, length us, event | category | flops | bytes accessed | tf_op | source)
XLA Modules:
  0.0 134.5 jit_solution(16829262492697275321)
XLA Ops:
  0.6 0.0 copy-start.2
  0.6 1.2 copy-done.2
  1.9 0.0 copy-start.4
  1.9 1.2 copy-done.4
  3.1 0.0 copy-start.6
  3.1 1.2 copy-done.6
  4.3 0.0 copy-start.8
  4.3 0.9 copy-done.8
  5.2 0.0 copy-start.10
  5.2 0.7 copy-done.10
  5.9 0.0 copy-start.12
  5.9 0.7 copy-done.12
  6.5 10.8 %shard_map.113 = (bf16[32,192,256]{2,1,0:T(8,128)(2,1)S(1)}, bf16[64,8192]{1,0:T(8,128)(2,1)S(1)}, bf16[1024,128]{1,0:T(8,128)(2,1)S(1)}) custom-call(bf16[2,32,64,128]{3,2,1,0:T(8,128)(2,1)S(1)} %copy-done.2, bf16[2,32,64,128]{3,2,1,0:T(8,128)(2,1)S(1)} %copy-done.4, bf16[2,32,64,128]{3,2,1,0:T(8,128)(2,1)S(1)} %copy-done.6, ...), custom_call_target="tpu_custom_call" | custom-call | flops 16777216 | bytes 8388608 | tf_op jit(solution)/shard_map/pallas_call | solution.py:223
  17.3 0.0 copy-start
  17.3 1.6 %copy-done = bf16[32,192,256]{2,1,0:T(8,128)(2,1)} copy-done((bf16[32,192,256]{2,1,0:T(8,128)(2,1)}, bf16[32,192,256]{2,1,0:T(8,128)(2,1)S(1)}, u32[]{:S(2)}) %copy-start) | copy-done | bytes 3145752
  18.9 0.0 copy-start.17
  18.9 1.0 copy-done.17
  19.9 0.0 copy-start.19
  19.9 0.7 copy-done.19
  20.6 0.0 copy-start.25
  20.6 7.5 %all-to-all-start = ((bf16[32,192,256]{2,1,0:T(8,128)(2,1)}), bf16[32,192,256]{2,1,0:T(8,128)(2,1)S(1)}, u32[]{:S(2)}, u32[]{:S(2)}) async-start(bf16[32,192,256]{2,1,0:T(8,128)(2,1)} %copy-done), calls=%async_computation | async-start | bytes 6291456 | tf_op jit(solution)/shard_map/all_to_all | solution.py:651
  28.1 0.0 copy-done.25
  28.1 0.2 reduce-window.8
  28.3 0.1 convert_reduce_fusion
  28.4 0.1 compare_select_fusion
  28.5 0.1 pad_maximum_fusion.mask
  28.6 1.9 %copy-done.1 = bf16[32,192,256]{2,1,0:T(8,128)(2,1)S(1)} copy-done((bf16[32,192,256]{2,1,0:T(8,128)(2,1)S(1)}, bf16[32,192,256]{2,1,0:T(8,128)(2,1)}, u32[]{:S(2)}) %copy-start.1) | copy-done | bytes 3145752
  30.5 1.2 copy-done.18
  31.7 0.9 copy-done.20
  32.6 37.9 %shard_map.114 = (bf16[1024,128]{1,0:T(8,128)(2,1)S(1)}, f32[4096,128]{1,0:T(8,128)S(1)}) custom-call(bf16[1024,128]{1,0:T(8,128)(2,1)S(1)} %copy-done.20, bf16[64,8192]{1,0:T(8,128)(2,1)S(1)} %copy-done.18, bf16[32,192,256]{2,1,0:T(8,128)(2,1)S(1)} %copy-done.1), custom_call_target="tpu_custom_call" | custom-call | flops 18253611008 | bytes 8388608 | tf_op jit(solution)/shard_map/pallas_call | solution.py:326
  70.5 0.0 copy-start.21
  70.5 1.4 %copy-done.21 = f32[4096,128]{1,0:T(8,128)} copy-done((f32[4096,128]{1,0:T(8,128)}, f32[4096,128]{1,0:T(8,128)S(1)}, u32[]{:S(2)}) %copy-start.21) | copy-done | bytes 2097176
  71.9 0.7 copy-done.23
  72.6 0.0 all-to-all-done.patch
  72.6 0.0 copy-done.9
  72.6 0.0 copy-done.13
  72.6 0.0 copy-start.3
  72.6 1.2 copy-done.3
  73.8 1.2 copy-done.5
  75.1 1.2 copy-done.7
  76.3 1.2 copy-done.16
  77.5 1.6 %copy-done.22 = f32[4096,128]{1,0:T(8,128)S(1)} copy-done((f32[4096,128]{1,0:T(8,128)S(1)}, f32[4096,128]{1,0:T(8,128)}, u32[]{:S(2)}) %copy-start.22) | copy-done | bytes 2097176
  79.1 0.9 copy-done.24
  80.1 52.6 %shard_map.115 = (f32[4096,128]{1,0:T(8,128)S(1)}, f32[8,32,128]{2,1,0:T(8,128)S(1)}, f32[16,32,128]{2,1,0:T(8,128)S(1)}, f32[32,128]{1,0:T(8,128)S(1)}) custom-call(bf16[32,192,256]{2,1,0:T(8,128)(2,1)S(1)} %all-to-all-done.patch, f32[64,128]{1,0:T(8,128)S(1)} %pad_maximum_fusion.mask, bf16[1024,128]{1,0:T(8,128)(2,1)S(1)} %copy-done.24, ...), custom_call_target="tpu_custom_call" | custom-call | flops 4294967296 | bytes 12582912 | tf_op jit(solution)/shard_map/pallas_call | solution.py:549
  132.6 0.0 copy-done.11
  132.7 0.0 copy-done.14
  132.7 0.0 copy-done.15
  132.7 1.9 %shard_map.116 = (bf16[2,32,64,128]{3,2,1,0:T(8,128)(2,1)}, bf16[16,32,128]{2,1,0:T(8,128)(2,1)}) custom-call(f32[4096,128]{1,0:T(8,128)S(1)} %get-tuple-element.22.acc, f32[8,32,128]{2,1,0:T(8,128)S(1)} %get-tuple-element.23.pall, f32[16,32,128]{2,1,0:T(8,128)S(1)} %get-tuple-element.24.irow, f32[32,128]{1,0:T(8,128)S(1)} %get-tuple-element.25.istat, ...), custom_call_target="tpu_custom_call" | custom-call | flops 4194304 | bytes 3145728 | tf_op jit(solution)/shard_map/pallas_call | solution.py:618
  (14 shorter events, 0.0 us)
Async XLA Ops:
  0.6 1.2 copy-start.2
  1.9 1.2 copy-start.4
  3.1 1.2 copy-start.6
  4.3 0.9 copy-start.8
  5.2 0.7 copy-start.10
  5.9 0.7 copy-start.12
  17.3 1.6 %copy-start = (bf16[32,192,256]{2,1,0:T(8,128)(2,1)}, bf16[32,192,256]{2,1,0:T(8,128)(2,1)S(1)}, u32[]{:S(2)}) copy-start(bf16[32,192,256]{2,1,0:T(8,128)(2,1)S(1)} %get-tuple-element.17.buf) | copy-start | bytes 9437188
  18.9 1.0 copy-start.17
  19.9 0.7 copy-start.19
  20.6 7.5 %copy-start.25 = (s32[4]{0:T(128)S(1)}, s32[4]{0:T(128)}, u32[]{:S(2)}) copy-start(s32[4]{0:T(128)} %param.10) | copy-start | bytes 52
  20.6 52.0 %all-to-all-start = ((bf16[32,192,256]{2,1,0:T(8,128)(2,1)}), bf16[32,192,256]{2,1,0:T(8,128)(2,1)S(1)}, u32[]{:S(2)}, u32[]{:S(2)}) async-start(bf16[32,192,256]{2,1,0:T(8,128)(2,1)} %copy-done), calls=%async_computation | async-start | bytes 6291456 | tf_op jit(solution)/shard_map/all_to_all | solution.py:651
  28.6 1.9 %copy-start.1 = (bf16[32,192,256]{2,1,0:T(8,128)(2,1)S(1)}, bf16[32,192,256]{2,1,0:T(8,128)(2,1)}, u32[]{:S(2)}) copy-start(bf16[32,192,256]{2,1,0:T(8,128)(2,1)} %copy-done) | copy-start | bytes 9437188
  30.5 1.2 copy-start.18
  31.7 0.9 copy-start.20
  32.6 40.0 %copy-start.9 = (bf16[128,16,32]{0,2,1:T(8,128)(2,1)S(1)}, bf16[128,16,32]{0,2,1:T(8,128)(2,1)}, u32[]{:S(2)}) copy-start(bf16[128,16,32]{0,2,1:T(8,128)(2,1)} %param.18) | copy-start | bytes 393220
  32.6 40.0 %copy-start.13 = (s32[128,1]{0,1:T(1,128)S(1)}, s32[128,1]{0,1:T(1,128)}, u32[]{:S(2)}) copy-start(s32[128,1]{0,1:T(1,128)} %param.11) | copy-start | bytes 1540
  70.5 1.4 %copy-start.21 = (f32[4096,128]{1,0:T(8,128)}, f32[4096,128]{1,0:T(8,128)S(1)}, u32[]{:S(2)}) copy-start(f32[4096,128]{1,0:T(8,128)S(1)} %get-tuple-element.21.wide) | copy-start | bytes 6291460
  71.9 0.7 copy-start.23
  72.6 1.2 copy-start.3
  73.8 1.2 copy-start.5
  75.1 1.2 copy-start.7
  76.3 1.2 copy-start.16
  77.5 1.6 %copy-start.22 = (f32[4096,128]{1,0:T(8,128)S(1)}, f32[4096,128]{1,0:T(8,128)}, u32[]{:S(2)}) copy-start(f32[4096,128]{1,0:T(8,128)} %copy-done.21) | copy-start | bytes 6291460
  79.1 0.9 copy-start.24
  80.1 52.6 %copy-start.11 = (s32[128]{0:T(128)S(1)}, s32[128]{0:T(128)}, u32[]{:S(2)}) copy-start(s32[128]{0:T(128)} %param.12) | copy-start | bytes 1540
  80.1 52.6 %copy-start.14 = (f32[32]{0:T(128)S(1)}, f32[32]{0:T(128)}, u32[]{:S(2)}) copy-start(f32[32]{0:T(128)} %pgain.1) | copy-start | bytes 388
  80.1 52.6 %copy-start.15 = (f32[32]{0:T(128)S(1)}, f32[32]{0:T(128)}, u32[]{:S(2)}) copy-start(f32[32]{0:T(128)} %param.19) | copy-start | bytes 388

commit v2 on v1

--- a/solution.py
+++ b/solution.py
@@ -19,6 +19,7 @@
 QROWS = 2048 + BIG
 VM = pl.BlockSpec(memory_space=pltpu.VMEM)
 SM = pl.BlockSpec(memory_space=pltpu.SMEM)
+HB = pl.BlockSpec(memory_space=pltpu.HBM)
 
 
 def rows_at(start, size):
@@ -72,7 +73,8 @@
                     buf[d, pl.ds(64 + f * 32, 32), lanes],
                     buf[d, pl.ds(128 + f * 32, 32), lanes],
                 )
-                acc[pl.ds(f * 2048 + d * 2 + half, 32, stride=64), :] = o
+                r = pl.ds(f * 2048 + d * 2 + half, 32, stride=64)
+                acc[r, :] = acc[r, :] + o
             return 0
 
         lax.fori_loop(0, 32, body, 0, unroll=unroll)
@@ -87,12 +89,12 @@
     lax.fori_loop(0, 32, body, 0, unroll=4)
 
 
-def height_out(os, features, wide, acc):
+def height_out(os, features, acc):
     def body(c, _):
         t = os[pl.ds(c, 128, stride=32), :].T
         for f in range(2):
             r = rows_at(f * 2048 + c * 64, 64)
-            acc[r, :] = wide[r, :] + t[f * 64 : (f + 1) * 64] + features[f, c].astype(F32)
+            acc[r, :] = t[f * 64 : (f + 1) * 64] + features[f, c].astype(F32)
         return 0
 
     lax.fori_loop(0, 32, body, 0, unroll=4)
@@ -145,10 +147,13 @@
 
 
 def first_kernel(
-    q, k, v, inst, trow, qrow, buf, kflat, got, stage, rows, msg, raw,
-    send_sem, recv_sem, own_sem, load_sem,
+    q, k, v, inst_hbm, trow, qrow, buf_hbm, kflat_hbm, got,
+    stage, rows, msg, raw, inst, buf, kflat,
+    send_sem, recv_sem, own_sem, load_sem, save_sem,
 ):
     me = lax.axis_index("st")
+    load_inst = pltpu.make_async_copy(inst_hbm, inst, load_sem.at[3])
+    load_inst.start()
     loads = []
     for number, src in enumerate((k, v, q)):
         load = pltpu.make_async_copy(src, raw.at[number], load_sem.at[number])
@@ -165,6 +170,7 @@
         (((1,), (1,)), ((), ())),
         preferred_element_type=F32,
     )
+    load_inst.wait()
     for r in range(16):
         x = inst[r].astype(F32)
         y = jnp.where(here, jnp.concatenate([x, x, x, x], axis=0), 0.0).astype(BF)
@@ -191,6 +197,7 @@
         msg.at[rows_at(me * 32, 32)], got.at[rows_at(me * 32, 32)], own_sem
     )
     own.start()
+    saves = []
     for number in range(3):
         base = (64, 128, 0)[number]
         loads[number].wait()
@@ -211,6 +218,18 @@
             return 0
 
         lax.fori_loop(0, 32, body, 0, unroll=4)
+        part = pl.ds(base, 64)
+        save = pltpu.make_async_copy(
+            buf.at[:, part, :], buf_hbm.at[:, part, :], save_sem.at[number]
+        )
+        save.start()
+        saves.append(save)
+        if number == 0:
+            save = pltpu.make_async_copy(kflat, kflat_hbm, save_sem.at[3])
+            save.start()
+            saves.append(save)
+    for save in saves:
+        save.wait()
     own.wait()
     for copy in copies:
         copy.wait()
@@ -219,24 +238,27 @@
 def first(q, k, v, inst, trow, qrow):
     sd = jax.ShapeDtypeStruct
     dma = pltpu.SemaphoreType.DMA
-    any_space = pl.BlockSpec(memory_space=pl.ANY)
     return pl.pallas_call(
         first_kernel,
         out_shape=(sd((32, 192, 256), BF), sd((64, 8192), BF), sd((1024, 128), BF)),
-        in_specs=[any_space] * 3 + [VM] * 3,
-        out_specs=(VM, VM, VM),
+        in_specs=[HB] * 4 + [VM] * 2,
+        out_specs=(HB, HB, HB),
         scratch_shapes=[
             pltpu.VMEM((4096, 128), F32),
             pltpu.VMEM((1024, 128), F32),
             pltpu.VMEM((1024, 128), BF),
             pltpu.VMEM((3, 2, 32, 64, 128), BF),
+            pltpu.VMEM((16, 32, 128), BF),
+            pltpu.VMEM((32, 192, 256), BF),
+            pltpu.VMEM((64, 8192), BF),
             dma((31,)),
             dma((31,)),
             dma,
-            dma((3,)),
+            dma((4,)),
+            dma((4,)),
         ],
         compiler_params=pltpu.CompilerParams(
-            collective_id=0, has_side_effects=True, vmem_limit_bytes=20 << 20
+            collective_id=0, has_side_effects=True, vmem_limit_bytes=60 << 20
         ),
         cost_estimate=pl.CostEstimate(flops=1 << 24, bytes_accessed=8 << 20, transcendentals=0),
     )(q, k, v, inst, trow, qrow)
@@ -253,30 +275,48 @@
         here = jnp.max(s, axis=1, keepdims=True) * SCALE2
         new = here if most is None else jnp.maximum(most, here)
         p = jnp.exp2(s * SCALE2 - new).astype(BF)
-        o = jnp.dot(p, values[f, pl.ds(j * CHUNK, CHUNK), :], preferred_element_type=F32)
+        o = jnp.dot(p, values[pl.ds(j * CHUNK, CHUNK), :], preferred_element_type=F32)
         acc = o if acc is None else acc * jnp.exp2(most - new) + o
         most = new
-    return acc / acc[:, 32:33]
-
-
-def cross_kernel(got, kflat, buf, ans, acc, values, wide, packed, solved, live, counts, starts, sem):
+    return acc / acc[:, 64:65]
+
+
+def middle_kernel(
+    got_hbm, kflat_hbm, buf_hbm, q, k, v, features, ans_hbm, wide_hbm,
+    got, kflat, buf, raw, ans, acc, qs, ks, vs, os,
+    values, wide, packed, solved, live, counts, starts, sem,
+):
+    pairs = ((got_hbm, got), (buf_hbm, buf)) + tuple(
+        (src, raw.at[i]) for i, src in enumerate((q, k, v, features))
+    ) + ((kflat_hbm, kflat),)
+    loads = [pltpu.make_async_copy(x, y, sem.at[i]) for i, (x, y) in enumerate(pairs)]
+    for load in loads:
+        load.start()
+    loads[0].wait()
     wide[...] = got[...].astype(F32)
     alive = jnp.where(wide[...] < DEAD / 2, 1.0, 0.0).reshape(64, 16, 128)
     live[...] = jnp.sum(alive, axis=1).astype(jnp.int32)
-    down = pltpu.make_async_copy(live, counts, sem)
+    down = pltpu.make_async_copy(live, counts, sem.at[7])
     down.start()
+    loads[1].wait()
 
     def turn(d, _):
-        for f in range(2):
-            t = buf[d, pl.ds(128 + f * 32, 32), :].astype(F32)
-            one = jnp.ones((32, 256), F32)
-            full = jnp.concatenate([t, one, one, one], axis=0)
-            values[f, rows_at(d * 256, 256), :] = full.T.astype(BF)
+        t = buf[d, pl.ds(128, 64), :].astype(F32)
+        full = jnp.concatenate([t, jnp.ones((64, 256), F32)], axis=0)
+        values[rows_at(d * 256, 256), :] = full.T.astype(BF)
         return 0
 
     lax.fori_loop(0, 32, turn, 0, unroll=2)
+    for load in loads[2:]:
+        load.wait()
+    height_in(raw.at[0], qs)
+    height_in(raw.at[1], ks)
+    height_in(raw.at[2], vs)
+    attend_pairs(qs, ks, vs, os, None, 128, 32)
+    height_out(os, raw.at[3], acc)
+    save = pltpu.make_async_copy(acc, wide_hbm, sem.at[8])
+    save.start()
     down.wait()
-    width_all(buf, acc, 8)
 
     for f in range(2):
 
@@ -289,7 +329,7 @@
                 offset = offset + counts[src * 2 + f, 32 * j]
             return offset
 
-        total = lax.fori_loop(0, 32, pack, 0)
+        total = lax.fori_loop(0, 32, pack, 0, unroll=4)
         many = (total + SMALL - 1) // BIG
         rest = jnp.maximum(total - many * BIG, 0)
 
@@ -313,39 +353,52 @@
             out = jnp.zeros((16, 128), F32)
             for j in range(4):
                 x = solved[pl.ds(starts[src * 2 + f, j], 16), :]
-                moved = x if j == 0 else pltpu.roll(x, 32 * j, 1)
+                shift = (32 * (j - f)) % 128
+                moved = x if shift == 0 else pltpu.roll(x, shift, 1)
                 keep = (group == j) & (row < counts[src * 2 + f, 32 * j])
                 out = jnp.where(keep, moved, out)
             ans[pl.ds(pl.multiple_of(src * 32 + f * 16, 16), 16), :] = out.astype(BF)
             return 0
 
-        lax.fori_loop(0, 32, unpack, 0)
-
-
-def cross(got, kflat, buf):
+        lax.fori_loop(0, 32, unpack, 0, unroll=4)
+    back = pltpu.make_async_copy(ans, ans_hbm, sem.at[9])
+    back.start()
+    back.wait()
+    save.wait()
+
+
+def middle(got, kflat, buf, q, k, v, features):
+    sd = jax.ShapeDtypeStruct
     return pl.pallas_call(
-        cross_kernel,
-        out_shape=(
-            jax.ShapeDtypeStruct((1024, 128), BF),
-            jax.ShapeDtypeStruct((4096, 128), F32),
-        ),
-        in_specs=[VM] * 3,
-        out_specs=(VM, VM),
+        middle_kernel,
+        out_shape=(sd((1024, 128), BF), sd((4096, 128), F32)),
+        in_specs=[HB] * 7,
+        out_specs=(HB, HB),
         scratch_shapes=[
-            pltpu.VMEM((2, 8192, 128), BF),
+            pltpu.VMEM((1024, 128), BF),
+            pltpu.VMEM((64, 8192), BF),
+            pltpu.VMEM((32, 192, 256), BF),
+            pltpu.VMEM((4, 2, 32, 64, 128), BF),
+            pltpu.VMEM((1024, 128), BF),
+            pltpu.VMEM((4096, 128), F32),
+            pltpu.VMEM((4096, 128), F32),
+            pltpu.VMEM((4096, 128), F32),
+            pltpu.VMEM((4096, 128), F32),
+            pltpu.VMEM((4096, 128), F32),
+            pltpu.VMEM((8192, 128), BF),
             pltpu.VMEM((1024, 128), F32),
             pltpu.VMEM((QROWS, 128), F32),
             pltpu.VMEM((QROWS, 128), F32),
             pltpu.VMEM((64, 128), jnp.int32),
             pltpu.SMEM((64, 128), jnp.int32),
             pltpu.SMEM((64, 4), jnp.int32),
-            pltpu.SemaphoreType.DMA,
+            pltpu.SemaphoreType.DMA((10,)),
         ],
-        compiler_params=pltpu.CompilerParams(vmem_limit_bytes=32 << 20),
+        compiler_params=pltpu.CompilerParams(vmem_limit_bytes=60 << 20),
         cost_estimate=pl.CostEstimate(
             flops=17 << 30, bytes_accessed=8 << 20, transcendentals=1 << 24
         ),
-    )(got, kflat, buf)
+    )(got, kflat, buf, q, k, v, features)
 
 
 def time_half(patch, mask, half, stage, qs, ks, vs, os, out):
@@ -368,7 +421,7 @@
             return 0
 
         lax.fori_loop(0, 16, turn, 0, unroll=4)
-    attend_pairs(qs, ks, vs, os, mask, 64, 16)
+    attend_pairs(qs, ks, vs, os, mask, 64, 32)
 
     def turn_back(b, _):
         one, two = pl.ds(b * 2, 64, stride=32), pl.ds(b * 2 + 1, 64, stride=32)
@@ -390,20 +443,19 @@
 
 
 def last_kernel(
-    patch, mask, ans, q, k, v, features, wide, inst, trow,
+    patch, mask, ans, wide, buf_hbm, inst, trow,
     acc, pall, irow, istat,
-    raw, timed, tback, aback, stage, qs, ks, vs, os, arow, part, partbf, pgot, pnew,
+    buf, timed, tback, aback, stage, qs, ks, vs, os, arow, part, partbf, pgot, pnew,
     ipart, igot, tsend, trecv, asend, arecv, own_sem, zsend, zrecv, load_sem,
 ):
     me = lax.axis_index("st")
     mz = lax.axis_index("ha")
     hello("st", 32)
     hello("ha", 8)
-    loads = []
-    for number, src in enumerate((q, k, v, features)):
-        load = pltpu.make_async_copy(src, raw.at[number], load_sem.at[number])
-        load.start()
-        loads.append(load)
+    load = pltpu.make_async_copy(wide, acc, load_sem.at[0])
+    load.start()
+    load_flat = pltpu.make_async_copy(buf_hbm, buf, load_sem.at[1])
+    load_flat.start()
 
     def to_st(src, dst, send, recv, i, peer):
         copy = pltpu.make_async_remote_copy(
@@ -452,13 +504,9 @@
     time_half(patch, known, 1, stage, qs, ks, vs, os, timed)
     backs = backs + return_half(1)
 
-    for load in loads:
-        load.wait()
-    height_in(raw.at[0], qs)
-    height_in(raw.at[1], ks)
-    height_in(raw.at[2], vs)
-    attend_pairs(qs, ks, vs, os, None, 128, 16)
-    height_out(os, raw.at[3], wide, acc)
+    load.wait()
+    load_flat.wait()
+    width_all(buf, acc, 16)
 
     def exchange(src, dst, at_src, at_dst, which):
         copies = []
@@ -534,43 +582,42 @@
     for z in range(1, 8):
         total = total + pgot[z].astype(F32)
     mean = total[:16] / C
-    pnew[0:16, :] = mean
-    pnew[16:32, :] = lax.rsqrt(total[16:] / C - mean * mean + EPSILON)
+    pnew[0:16, :] = mean.astype(BF)
+    pnew[16:32, :] = lax.rsqrt(total[16:] / C - mean * mean + EPSILON).astype(BF)
     gathered = exchange(pnew, pall, lambda a, p: a, lambda a: a.at[mz], 2)
     pall[mz] = pnew[...]
     for copy in gathered:
         copy.wait()
 
 
-def last(patch, mask, ans, q, k, v, features, wide, inst, trow):
+def last(patch, mask, ans, wide, buf, inst, trow):
     sd = jax.ShapeDtypeStruct
     dma = pltpu.SemaphoreType.DMA
-    any_space = pl.BlockSpec(memory_space=pl.ANY)
     return pl.pallas_call(
         last_kernel,
         out_shape=(
             sd((4096, 128), F32),
-            sd((8, 32, 128), F32),
+            sd((8, 32, 128), BF),
             sd((16, 32, 128), F32),
             sd((32, 128), F32),
         ),
-        in_specs=[VM] * 3 + [any_space] * 4 + [VM] * 3,
+        in_specs=[VM] * 2 + [HB] * 3 + [VM] * 2,
         out_specs=(VM, VM, VM, VM),
         scratch_shapes=[
-            pltpu.VMEM((4, 2, 32, 64, 128), BF),
+            pltpu.VMEM((32, 192, 256), BF),
             pltpu.VMEM((2, 32, 64, 128), BF),
             pltpu.VMEM((2, 32, 64, 128), BF),
             pltpu.VMEM((1024, 128), BF),
             pltpu.VMEM((2048, 128), F32),
-            pltpu.VMEM((4096, 128), F32),
-            pltpu.VMEM((4096, 128), F32),
-            pltpu.VMEM((4096, 128), F32),
-            pltpu.VMEM((4096, 128), F32),
+            pltpu.VMEM((2048, 128), F32),
+            pltpu.VMEM((2048, 128), F32),
+            pltpu.VMEM((2048, 128), F32),
+            pltpu.VMEM((2048, 128), F32),
             pltpu.VMEM((1024, 128), F32),
             pltpu.VMEM((8, 32, 128), F32),
             pltpu.VMEM((8, 32, 128), BF),
             pltpu.VMEM((8, 32, 128), BF),
-            pltpu.VMEM((32, 128), F32),
+            pltpu.VMEM((32, 128), BF),
             pltpu.VMEM((32, 128), F32),
             pltpu.VMEM((8, 32, 128), F32),
             dma((2, 31)),
@@ -580,19 +627,36 @@
             dma((3,)),
             dma((3, 8)),
             dma((3, 8)),
-            dma((4,)),
+            dma((2,)),
         ],
         compiler_params=pltpu.CompilerParams(
-            collective_id=1, has_side_effects=True, vmem_limit_bytes=34 << 20
+            collective_id=1, has_side_effects=True, vmem_limit_bytes=60 << 20
         ),
         cost_estimate=pl.CostEstimate(
             flops=1 << 32, bytes_accessed=12 << 20, transcendentals=1 << 21
         ),
-    )(patch, mask, ans, q, k, v, features, wide, inst, trow)
-
-
-def norm_kernel(acc, pall, irow, istat, qrow, pgain, igain, pixel_out, inst_out):
+    )(patch, mask, ans, wide, buf, inst, trow)
+
+
+def norm_kernel(
+    acc_hbm, pall_hbm, irow_hbm, istat_hbm, qrow, pgain, igain, pixel_hbm, inst_out,
+    acc, pall, irow, istat, pixel_out, sem,
+):
+    loads = [
+        pltpu.make_async_copy(pall_hbm, pall, sem.at[0]),
+        pltpu.make_async_copy(acc_hbm.at[pl.ds(0, 2048)], acc.at[pl.ds(0, 2048)], sem.at[1]),
+        pltpu.make_async_copy(
+            acc_hbm.at[pl.ds(2048, 2048)], acc.at[pl.ds(2048, 2048)], sem.at[2]
+        ),
+        pltpu.make_async_copy(istat_hbm, istat, sem.at[3]),
+        pltpu.make_async_copy(irow_hbm, irow, sem.at[4]),
+    ]
+    for load in loads:
+        load.start()
+    loads[0].wait()
+    saves = []
     for f in range(2):
+        loads[1 + f].wait()
 
         def finish(c, _):
             r = rows_at(f * 2048 + c * 64, 64)
@@ -600,17 +664,25 @@
             x = acc[r, :]
             for b in range(4):
                 low = slice(b * 16, (b + 1) * 16)
-                y = (x[low] - pall[f * 4 + b, 0:16, :]) * pall[f * 4 + b, 16:32, :] * gain
+                known = pall[f * 4 + b].astype(F32)
+                y = (x[low] - known[:16]) * known[16:] * gain
                 pixel_out[f, c, low, :] = y.astype(BF)
             return 0
 
         lax.fori_loop(0, 32, finish, 0, unroll=4)
+        save = pltpu.make_async_copy(pixel_out.at[f], pixel_hbm.at[f], sem.at[5 + f])
+        save.start()
+        saves.append(save)
+    loads[3].wait()
+    loads[4].wait()
     row = igain[...]
     gains = columns_of(jnp.concatenate([row, row, row, row], axis=1))[:32]
     live = qrow[...]
     for r in range(16):
         y = (irow[r] - istat[pl.ds(r, 1), :]) * istat[pl.ds(16 + r, 1), :] * gains
         inst_out[r] = jnp.where(live > r, y, 0.0).astype(BF)
+    for save in saves:
+        save.wait()
 
 
 def norm(acc, pall, irow, istat, qrow, pgain, igain):
@@ -618,9 +690,17 @@
     return pl.pallas_call(
         norm_kernel,
         out_shape=(sd((2, 32, 64, 128), BF), sd((16, 32, 128), BF)),
-        in_specs=[VM] * 5 + [SM, VM],
-        out_specs=(VM, VM),
-        compiler_params=pltpu.CompilerParams(vmem_limit_bytes=12 << 20),
+        in_specs=[HB] * 4 + [VM, SM, VM],
+        out_specs=(HB, VM),
+        scratch_shapes=[
+            pltpu.VMEM((4096, 128), F32),
+            pltpu.VMEM((8, 32, 128), BF),
+            pltpu.VMEM((16, 32, 128), F32),
+            pltpu.VMEM((32, 128), F32),
+            pltpu.VMEM((2, 32, 64, 128), BF),
+            pltpu.SemaphoreType.DMA((7,)),
+        ],
+        compiler_params=pltpu.CompilerParams(vmem_limit_bytes=60 << 20),
         cost_estimate=pl.CostEstimate(flops=1 << 22, bytes_accessed=3 << 20, transcendentals=0),
     )(acc, pall, irow, istat, qrow, pgain, igain)
 
@@ -649,10 +729,8 @@
     buf, kflat, got = first(pix_q, pix_k, pix_v, inst, trow, qrow)
     buf, got = lax.optimization_barrier((buf, got))
     patch = lax.all_to_all(buf, "st", split_axis=0, concat_axis=0, tiled=True)
-    ans, wide = cross(got, kflat, buf)
-    acc, pall, irow, istat = last(
-        patch, mask, ans, pix_q, pix_k, pix_v, features, wide, inst, trow
-    )
+    ans, wide = middle(got, kflat, buf, pix_q, pix_k, pix_v, features)
+    acc, pall, irow, istat = last(patch, mask, ans, wide, buf, inst, trow)
     pixel_out, inst_out = norm(
         acc, pall, irow, istat, qrow, pixel_gain, inst_gain.reshape(1, 32)
     )

time: 135 us -> 115 us (0.85)
  local copies, waits for them, and re-layouts: 22.8 us -> 1.69 us
  Pallas kernels: 103 us -> 99 us
  waiting for transfers between devices: 0.01 us -> 3.93 us
    unnamed x52 -> x4, local copies, waits for them, and re-layouts: 22.8 us -> 1.69 us
    pallas_call x1, Pallas kernels: 37.9 us -> 31.5 us  [middle(): pl.pallas_call(middle_kernel, out_shape=(sd((1024, 128), BF), sd((4096, 1...]
    all_to_all x1, waiting for transfers between devices: 0.01 us -> 3.93 us  [per_device(): patch = lax.all_to_all(buf, 'st', split_axis=0, concat_axis=0, tiled=True)]
    pallas_call x1, Pallas kernels: 1.88 us -> 4.05 us  [norm(): pl.pallas_call(norm_kernel, out_shape=(sd((2, 32, 64, 128), BF), sd((16,...]
  transfers between devices with their start and end apart: 1 -> 1, of which waited for: 0 -> 1; matrix products, arithmetic and copies ran while one was open for 0% -> 1% of each run, Pallas kernels for 28% -> 28%
where the time goes in v2:
time: 115 us; the launch traced here: 114 us
  Pallas kernels  99 us (86%)
  starting transfers between devices  7.41 us (6%)
  waiting for transfers between devices  3.93 us (3%)
  local copies, waits for them, and re-layouts  1.69 us (1%)
    pallas_call x1, Pallas kernels, last(): pl.pallas_call(last_kernel, out_shape=(sd((4096, 128), F32), sd((8, 32, 1...  52.1 us
    pallas_call x1, Pallas kernels, middle(): pl.pallas_call(middle_kernel, out_shape=(sd((1024, 128), BF), sd((4096, 1...  31.5 us
    pallas_call x1, Pallas kernels, first(): pl.pallas_call(first_kernel, out_shape=(sd((32, 192, 256), BF), sd((64, 8...  11.3 us
    all_to_all x1, starting transfers between devices, per_device(): patch = lax.all_to_all(buf, 'st', split_axis=0, concat_axis=0, tiled=True)  7.41 us
    pallas_call x1, Pallas kernels, norm(): pl.pallas_call(norm_kernel, out_shape=(sd((2, 32, 64, 128), BF), sd((16,...  4.05 us
    all_to_all x1, waiting for transfers between devices, per_device(): patch = lax.all_to_all(buf, 'st', split_axis=0, concat_axis=0, tiled=True)  3.93 us
  transfers between devices with their start and end apart: 1, of which 1 were waited for; matrix products, arithmetic and copies ran while one was open for 1% of the time, Pallas kernels for 28%

profile of v2, /device:TPU:14, one launch (start us, length us, event | category | flops | bytes accessed | tf_op | source)
XLA Modules:
  0.0 113.9 jit_solution(9365772051355016018)
XLA Ops:
  0.6 11.3 %shard_map.113 = (bf16[32,192,256]{2,1,0:T(8,128)(2,1)}, bf16[64,8192]{1,0:T(8,128)(2,1)}, bf16[1024,128]{1,0:T(8,128)(2,1)}) custom-call(bf16[2,32,64,128]{3,2,1,0:T(8,128)(2,1)} %q.3, bf16[2,32,64,128]{3,2,1,0:T(8,128)(2,1)} %k.3, bf16[2,32,64,128]{3,2,1,0:T(8,128)(2,1)} %v.3, bf16[16,32,128]{2,1,0:T(8,128)(2,1)} %bitcast.7, s32[1,128]{1,0:T(1,128)} %bitcast.11, ...), custom_call_target="tpu_custom_call" | custom-call | flops 16777216 | bytes 8388608 | tf_op jit(solution)/shard_map/pallas_call | solution.py:241
  12.0 0.0 copy-start.1
  12.0 7.4 %all-to-all-start = ((bf16[32,192,256]{2,1,0:T(8,128)(2,1)}), bf16[32,192,256]{2,1,0:T(8,128)(2,1)S(1)}, u32[]{:S(2)}, u32[]{:S(2)}) async-start(bf16[32,192,256]{2,1,0:T(8,128)(2,1)} %get-tuple-element.17.buf_hbm), calls=%async_computation | async-start | bytes 6291456 | tf_op jit(solution)/shard_map/all_to_all | solution.py:731
  19.4 0.0 copy-done.1
  19.4 0.2 reduce-window.8
  19.6 0.1 convert_reduce_fusion
  19.7 0.1 compare_select_fusion
  19.7 0.7 pad_maximum_fusion.mask
  20.4 31.5 %shard_map.114 = (bf16[1024,128]{1,0:T(8,128)(2,1)}, f32[4096,128]{1,0:T(8,128)}) custom-call(bf16[1024,128]{1,0:T(8,128)(2,1)} %get-tuple-element.18.got_hbm, bf16[64,8192]{1,0:T(8,128)(2,1)} %get-tuple-element.19.kflat_hbm, bf16[32,192,256]{2,1,0:T(8,128)(2,1)} %get-tuple-element.17.buf_hbm, bf16[2,32,64,128]{3,2,1,0:T(8,128)(2,1)} %q.3, ...), custom_call_target="tpu_custom_call" | custom-call | flops 18253611008 | bytes 8388608 | tf_op jit(solution)/shard_map/pallas_call | solution.py:372
  51.9 3.9 %all-to-all-done.patch = bf16[32,192,256]{2,1,0:T(8,128)(2,1)S(1)} async-done(((bf16[32,192,256]{2,1,0:T(8,128)(2,1)}), bf16[32,192,256]{2,1,0:T(8,128)(2,1)S(1)}, u32[]{:S(2)}, u32[]{:S(2)}) %all-to-all-start) | async-done | bytes 3145760 | tf_op jit(solution)/shard_map/all_to_all | solution.py:731
  55.9 0.0 copy-start
  55.9 1.7 %copy-done = bf16[32,192,256]{2,1,0:T(8,128)(2,1)} copy-done((bf16[32,192,256]{2,1,0:T(8,128)(2,1)}, bf16[32,192,256]{2,1,0:T(8,128)(2,1)S(1)}, u32[]{:S(2)}) %copy-start) | copy-done | bytes 3145752
  57.5 52.1 %shard_map.115 = (f32[4096,128]{1,0:T(8,128)}, bf16[8,32,128]{2,1,0:T(8,128)(2,1)}, f32[16,32,128]{2,1,0:T(8,128)}, f32[32,128]{1,0:T(8,128)}) custom-call(bf16[32,192,256]{2,1,0:T(8,128)(2,1)} %copy-done, f32[64,128]{1,0:T(8,128)} %pad_maximum_fusion.mask, bf16[1024,128]{1,0:T(8,128)(2,1)} %get-tuple-element.20.ans, f32[4096,128]{1,0:T(8,128)} %get-tuple-element.21.wide, ...), custom_call_target="tpu_custom_call" | custom-call | flops 4294967296 | bytes 12582912 | tf_op jit(solution)/shard_map/pallas_call | solution.py:596
  109.7 4.1 %shard_map.116 = (bf16[2,32,64,128]{3,2,1,0:T(8,128)(2,1)}, bf16[16,32,128]{2,1,0:T(8,128)(2,1)}) custom-call(f32[4096,128]{1,0:T(8,128)} %get-tuple-element.22.acc_hbm, bf16[8,32,128]{2,1,0:T(8,128)(2,1)} %get-tuple-element.23.pall_hbm, f32[16,32,128]{2,1,0:T(8,128)} %get-tuple-element.24.irow_hbm, f32[32,128]{1,0:T(8,128)} %get-tuple-element.25.istat_hbm, ...), custom_call_target="tpu_custom_call" | custom-call | flops 4194304 | bytes 3145728 | tf_op jit(solution)/shard_map/pallas_call | solution.py:690
Async XLA Ops:
  12.0 7.4 %copy-start.1 = (s32[4]{0:T(128)S(1)}, s32[4]{0:T(128)}, u32[]{:S(2)}) copy-start(s32[4]{0:T(128)} %param.10) | copy-start | bytes 52
  12.0 43.9 %all-to-all-start = ((bf16[32,192,256]{2,1,0:T(8,128)(2,1)}), bf16[32,192,256]{2,1,0:T(8,128)(2,1)S(1)}, u32[]{:S(2)}, u32[]{:S(2)}) async-start(bf16[32,192,256]{2,1,0:T(8,128)(2,1)} %get-tuple-element.17.buf_hbm), calls=%async_computation | async-start | bytes 6291456 | tf_op jit(solution)/shard_map/all_to_all | solution.py:731
  55.9 1.7 %copy-start = (bf16[32,192,256]{2,1,0:T(8,128)(2,1)}, bf16[32,192,256]{2,1,0:T(8,128)(2,1)S(1)}, u32[]{:S(2)}) copy-start(bf16[32,192,256]{2,1,0:T(8,128)(2,1)S(1)} %all-to-all-done.patch) | copy-start | bytes 9437188

commit v3 on v2

--- a/solution.py
+++ b/solution.py
@@ -401,7 +401,7 @@
     )(got, kflat, buf, q, k, v, features)
 
 
-def time_half(patch, mask, half, stage, qs, ks, vs, os, out):
+def time_half(patch, mask, half, stage, qs, ks, vs, os, out, between):
     low = lax.broadcasted_iota(jnp.int32, (64, 128), 1) < 64
     lanes = pl.ds(half * 128, 128)
     for base, dst in ((0, qs), (64, ks), (128, vs)):
@@ -421,6 +421,7 @@
             return 0
 
         lax.fori_loop(0, 16, turn, 0, unroll=4)
+    between()
     attend_pairs(qs, ks, vs, os, mask, 64, 32)
 
     def turn_back(b, _):
@@ -484,24 +485,27 @@
         return copies + [own]
 
     known = mask[...]
-    time_half(patch, known, 0, stage, qs, ks, vs, os, timed)
-    greeted(38)
     answers = []
-    for i, move in enumerate(MOVES):
-        peer = peer_to(me, move)
-        answers.append(
-            to_st(
-                ans.at[rows_at(peer * 32, 32)], aback.at[rows_at(me * 32, 32)],
-                asend, arecv, i, peer,
+
+    def send_answers():
+        greeted(38)
+        for i, move in enumerate(MOVES):
+            peer = peer_to(me, move)
+            answers.append(
+                to_st(
+                    ans.at[rows_at(peer * 32, 32)], aback.at[rows_at(me * 32, 32)],
+                    asend, arecv, i, peer,
+                )
             )
-        )
-    own = pltpu.make_async_copy(
-        ans.at[rows_at(me * 32, 32)], aback.at[rows_at(me * 32, 32)], own_sem.at[2]
-    )
-    own.start()
-    answers.append(own)
+        own = pltpu.make_async_copy(
+            ans.at[rows_at(me * 32, 32)], aback.at[rows_at(me * 32, 32)], own_sem.at[2]
+        )
+        own.start()
+        answers.append(own)
+
+    time_half(patch, known, 0, stage, qs, ks, vs, os, timed, send_answers)
     backs = return_half(0)
-    time_half(patch, known, 1, stage, qs, ks, vs, os, timed)
+    time_half(patch, known, 1, stage, qs, ks, vs, os, timed, lambda: None)
     backs = backs + return_half(1)
 
     load.wait()

time: 115 us -> 116 us (level)
  no operation moved by 1% of the time
where the time goes in v3:
time: 116 us; the launch traced here: 114 us
  Pallas kernels  98.9 us (85%)
  starting transfers between devices  7.41 us (6%)
  waiting for transfers between devices  3.93 us (3%)
  local copies, waits for them, and re-layouts  1.69 us (1%)
    pallas_call x1, Pallas kernels, last(): pl.pallas_call(last_kernel, out_shape=(sd((4096, 128), F32), sd((8, 32, 1...  52 us
    pallas_call x1, Pallas kernels, middle(): pl.pallas_call(middle_kernel, out_shape=(sd((1024, 128), BF), sd((4096, 1...  31.5 us
    pallas_call x1, Pallas kernels, first(): pl.pallas_call(first_kernel, out_shape=(sd((32, 192, 256), BF), sd((64, 8...  11.3 us
    all_to_all x1, starting transfers between devices, per_device(): patch = lax.all_to_all(buf, 'st', split_axis=0, concat_axis=0, tiled=True)  7.41 us
    pallas_call x1, Pallas kernels, norm(): pl.pallas_call(norm_kernel, out_shape=(sd((2, 32, 64, 128), BF), sd((16,...  4.05 us
    all_to_all x1, waiting for transfers between devices, per_device(): patch = lax.all_to_all(buf, 'st', split_axis=0, concat_axis=0, tiled=True)  3.93 us
  transfers between devices with their start and end apart: 1, of which 1 were waited for; matrix products, arithmetic and copies ran while one was open for 1% of the time, Pallas kernels for 28%

profile of v3, /device:TPU:14, one launch (start us, length us, event | category | flops | bytes accessed | tf_op | source)
XLA Modules:
  0.0 113.8 jit_solution(65691313124095471)
XLA Ops:
  0.6 11.3 %shard_map.113 = (bf16[32,192,256]{2,1,0:T(8,128)(2,1)}, bf16[64,8192]{1,0:T(8,128)(2,1)}, bf16[1024,128]{1,0:T(8,128)(2,1)}) custom-call(bf16[2,32,64,128]{3,2,1,0:T(8,128)(2,1)} %q.3, bf16[2,32,64,128]{3,2,1,0:T(8,128)(2,1)} %k.3, bf16[2,32,64,128]{3,2,1,0:T(8,128)(2,1)} %v.3, bf16[16,32,128]{2,1,0:T(8,128)(2,1)} %bitcast.7, s32[1,128]{1,0:T(1,128)} %bitcast.11, ...), custom_call_target="tpu_custom_call" | custom-call | flops 16777216 | bytes 8388608 | tf_op jit(solution)/shard_map/pallas_call | solution.py:241
  12.0 0.0 copy-start.1
  12.0 7.4 %all-to-all-start = ((bf16[32,192,256]{2,1,0:T(8,128)(2,1)}), bf16[32,192,256]{2,1,0:T(8,128)(2,1)S(1)}, u32[]{:S(2)}, u32[]{:S(2)}) async-start(bf16[32,192,256]{2,1,0:T(8,128)(2,1)} %get-tuple-element.17.buf_hbm), calls=%async_computation | async-start | bytes 6291456 | tf_op jit(solution)/shard_map/all_to_all | solution.py:735
  19.4 0.0 copy-done.1
  19.4 0.2 reduce-window.8
  19.6 0.1 convert_reduce_fusion
  19.7 0.1 compare_select_fusion
  19.7 0.7 pad_maximum_fusion.mask
  20.4 31.5 %shard_map.114 = (bf16[1024,128]{1,0:T(8,128)(2,1)}, f32[4096,128]{1,0:T(8,128)}) custom-call(bf16[1024,128]{1,0:T(8,128)(2,1)} %get-tuple-element.18.got_hbm, bf16[64,8192]{1,0:T(8,128)(2,1)} %get-tuple-element.19.kflat_hbm, bf16[32,192,256]{2,1,0:T(8,128)(2,1)} %get-tuple-element.17.buf_hbm, bf16[2,32,64,128]{3,2,1,0:T(8,128)(2,1)} %q.3, ...), custom_call_target="tpu_custom_call" | custom-call | flops 18253611008 | bytes 8388608 | tf_op jit(solution)/shard_map/pallas_call | solution.py:372
  51.9 3.9 %all-to-all-done.patch = bf16[32,192,256]{2,1,0:T(8,128)(2,1)S(1)} async-done(((bf16[32,192,256]{2,1,0:T(8,128)(2,1)}), bf16[32,192,256]{2,1,0:T(8,128)(2,1)S(1)}, u32[]{:S(2)}, u32[]{:S(2)}) %all-to-all-start) | async-done | bytes 3145760 | tf_op jit(solution)/shard_map/all_to_all | solution.py:735
  55.9 0.0 copy-start
  55.9 1.7 %copy-done = bf16[32,192,256]{2,1,0:T(8,128)(2,1)} copy-done((bf16[32,192,256]{2,1,0:T(8,128)(2,1)}, bf16[32,192,256]{2,1,0:T(8,128)(2,1)S(1)}, u32[]{:S(2)}) %copy-start) | copy-done | bytes 3145752
  57.5 52.0 %shard_map.115 = (f32[4096,128]{1,0:T(8,128)}, bf16[8,32,128]{2,1,0:T(8,128)(2,1)}, f32[16,32,128]{2,1,0:T(8,128)}, f32[32,128]{1,0:T(8,128)}) custom-call(bf16[32,192,256]{2,1,0:T(8,128)(2,1)} %copy-done, f32[64,128]{1,0:T(8,128)} %pad_maximum_fusion.mask, bf16[1024,128]{1,0:T(8,128)(2,1)} %get-tuple-element.20.ans, f32[4096,128]{1,0:T(8,128)} %get-tuple-element.21.wide, ...), custom_call_target="tpu_custom_call" | custom-call | flops 4294967296 | bytes 12582912 | tf_op jit(solution)/shard_map/pallas_call | solution.py:600
  109.6 4.1 %shard_map.116 = (bf16[2,32,64,128]{3,2,1,0:T(8,128)(2,1)}, bf16[16,32,128]{2,1,0:T(8,128)(2,1)}) custom-call(f32[4096,128]{1,0:T(8,128)} %get-tuple-element.22.acc_hbm, bf16[8,32,128]{2,1,0:T(8,128)(2,1)} %get-tuple-element.23.pall_hbm, f32[16,32,128]{2,1,0:T(8,128)} %get-tuple-element.24.irow_hbm, f32[32,128]{1,0:T(8,128)} %get-tuple-element.25.istat_hbm, ...), custom_call_target="tpu_custom_call" | custom-call | flops 4194304 | bytes 3145728 | tf_op jit(solution)/shard_map/pallas_call | solution.py:694
Async XLA Ops:
  12.0 7.4 %copy-start.1 = (s32[4]{0:T(128)S(1)}, s32[4]{0:T(128)}, u32[]{:S(2)}) copy-start(s32[4]{0:T(128)} %param.10) | copy-start | bytes 52
  12.0 43.9 %all-to-all-start = ((bf16[32,192,256]{2,1,0:T(8,128)(2,1)}), bf16[32,192,256]{2,1,0:T(8,128)(2,1)S(1)}, u32[]{:S(2)}, u32[]{:S(2)}) async-start(bf16[32,192,256]{2,1,0:T(8,128)(2,1)} %get-tuple-element.17.buf_hbm), calls=%async_computation | async-start | bytes 6291456 | tf_op jit(solution)/shard_map/all_to_all | solution.py:735
  55.9 1.7 %copy-start = (bf16[32,192,256]{2,1,0:T(8,128)(2,1)}, bf16[32,192,256]{2,1,0:T(8,128)(2,1)S(1)}, u32[]{:S(2)}) copy-start(bf16[32,192,256]{2,1,0:T(8,128)(2,1)S(1)} %all-to-all-done.patch) | copy-start | bytes 9437188
